TPU v7x, 32 devices: a whole 2x2x4 slice. The times are simulated.
32 devices in a mesh: shot: 2 (over x), slab: 16 (over z, y, core).
Axes of the slice: x: 2, y: 2, z: 4, core: 2. Of those that a mesh axis runs over, the one named last changes fastest.
Arguments:
- fwd_last: float32 [2, 256, 64, 128], P('shot', 'slab'), may hold values from -6 to 6
- fwd_prev: float32 [2, 256, 64, 128], P('shot', 'slab'), may hold values from -6 to 6
- velocity: float32 [256, 64, 128], P('slab'), may hold values from 0.5 to 1
- aperture: int32 [2, 64, 128], P('shot'), may hold values 0 or 1
- rec_index: int32 [2, 2048], P('shot'), may hold values from 0 to 2097151
- src_index: int32 [2], P('shot'), may hold values from 0 to 2097151
- residual: float32 [2, 32, 2048], P('shot'), may hold values from -6 to 6
Outputs:
- gradient: float32 [256, 64, 128], P('slab', 'shot')
- adjoint_field: float32 [2, 256, 64, 128], P('shot', 'slab')
All inputs are finite; a program needn't handle non-finite values. No bound on the sum of `aperture` on one device may be relied on, other than what follows from the above.
Results may differ from a plain program's by a relative error of at most 0.000025.
Values sent between devices are 32-bit elements; how exact they have to be, the bound alone decides.
No kernel may reach another device: no remote copies, remote signals or barrier semaphores. Data moves between devices by JAX's collectives and lax.ppermute only.
A program may use at most 256 MiB of HBM per device.

v0:
```python
import jax
import jax.numpy as jnp
from jax import lax
from jax.sharding import PartitionSpec as P

COEFS = (-205.0 / 72.0, 8.0 / 5.0, -1.0 / 5.0, 8.0 / 315.0, -1.0 / 560.0)
BLOCK_STEPS = 8


def with_halo(array, sides, width):
    for axis, dim in sides:
        count, length = (lax.axis_size(axis), array.shape[dim])
        up = [(i, (i + 1) % count) for i in range(count - 1)]
        down = [(j, i) for i, j in up]
        last = lax.slice_in_dim(array, length - width, length, axis=dim)
        initial = lax.slice_in_dim(array, 0, width, axis=dim)
        before = lax.ppermute(last, axis, up)
        after = lax.ppermute(initial, axis, down)
        array = jnp.concatenate([before, array, after], axis=dim)
    return array


def second_diff(padded, lower, count):
    centre = padded[:, lower : lower + count]
    total = 3.0 * COEFS[0] * centre
    for k in range(1, 5):
        total = total + COEFS[k] * (
            padded[:, lower + k : lower + k + count] + padded[:, lower - k : lower - k + count]
        )
    width_x = centre.shape[2]
    width_y = centre.shape[3]
    sides = jnp.pad(centre, ((0, 0), (0, 0), (4, 4), (4, 4)))
    for k in range(1, 5):
        total = total + COEFS[k] * (
            sides[:, :, 4 + k : 4 + k + width_x, 4 : 4 + width_y]
            + sides[:, :, 4 - k : 4 - k + width_x, 4 : 4 + width_y]
        )
    for k in range(1, 5):
        total = total + COEFS[k] * (
            sides[:, :, 4 : 4 + width_x, 4 + k : 4 + k + width_y]
            + sides[:, :, 4 : 4 + width_x, 4 - k : 4 - k + width_y]
        )
    return total


def ricker(step):
    arg = (jnp.pi * 0.06 * (step - 10.0)) ** 2
    return 10.0 * (1.0 - 2.0 * arg) * jnp.exp(-arg)


def on_device(fwd_last, fwd_prev, velocity, aperture, rec_index, src_index, residual):
    shots, depth, width_x, width_y = fwd_last.shape
    total_steps = residual.shape[1]
    plane = width_x * width_y
    ext_layers = depth + 8
    start_cell = lax.axis_index("slab") * depth * plane
    ext_base = start_cell - 4 * plane
    coef = (0.4 * velocity) ** 2
    gate_f = aperture.astype(jnp.float32)[:, None]
    cell_ids = jnp.arange(ext_layers * plane, dtype=jnp.int32)
    src_local = src_index - ext_base
    rec_local = rec_index - ext_base
    rec_valid = (rec_local >= 0) & (rec_local < ext_layers * plane)
    rec_local = jnp.where(rec_valid, rec_local, 0)
    shot_rows = jnp.broadcast_to(jnp.arange(shots, dtype=jnp.int32)[:, None], rec_local.shape)

    def rec_table(lowest):
        traces = lax.dynamic_slice_in_dim(residual, lowest, BLOCK_STEPS, 1)
        values = jnp.where(rec_valid[:, :, None], jnp.transpose(traces, (0, 2, 1)), 0.0)
        table = (
            jnp.zeros((shots, ext_layers * plane, BLOCK_STEPS), jnp.float32)
            .at[shot_rows, rec_local]
            .add(values)
        )
        return jnp.transpose(table, (0, 2, 1))

    def sources(step, table, lowest):
        wave = ricker(step.astype(jnp.float32))
        u_part = jnp.where(cell_ids[None, :] == src_local[:, None], wave, 0.0)
        l_part = lax.dynamic_index_in_dim(table, step - lowest, 1, keepdims=False)
        both = jnp.concatenate([u_part, l_part], axis=0).reshape(
            2 * shots, ext_layers, width_x, width_y
        )
        return both[:, 4 : 4 + depth]

    def term(u_cur, l_next, l_cur, l_new):
        return jnp.sum(gate_f * u_cur * (l_next - 2.0 * l_cur + l_new), axis=0)

    def block_run(b, carry):
        lowest = total_steps - BLOCK_STEPS - BLOCK_STEPS * b
        table = rec_table(lowest)

        def one_step(k, carry):
            nxt, cur, acc = carry
            step = total_steps - 1 - k
            padded = with_halo(cur, (("slab", 1),), 4)
            lap_now = second_diff(padded, 4, depth)
            fresh = 2.0 * cur - nxt + coef * (lap_now + sources(step, table, lowest))
            acc = acc + term(cur[:shots], nxt[shots:], cur[shots:], fresh[shots:])
            return (cur, fresh, acc)

        return lax.fori_loop(BLOCK_STEPS * b, BLOCK_STEPS * b + BLOCK_STEPS, one_step, carry)

    zero_l = jnp.zeros_like(fwd_last)
    nxt0 = jnp.concatenate([fwd_last, zero_l], axis=0)
    cur0 = jnp.concatenate([fwd_prev, zero_l], axis=0)
    zero_g = jnp.zeros((depth, width_x, width_y), jnp.float32)
    final = lax.fori_loop(
        0 // BLOCK_STEPS, total_steps // BLOCK_STEPS, block_run, (nxt0, cur0, zero_g)
    )
    summed = lax.psum_scatter(final[2], "shot", scatter_dimension=1, tiled=True)
    block = width_x // lax.axis_size("shot")
    speed_blk = lax.dynamic_slice_in_dim(velocity, lax.axis_index("shot") * block, block, 1)
    gradient = -2.0 / speed_blk * summed
    adjoint_field = final[1][shots:]
    return (gradient, adjoint_field)


def solution(mesh):
    in_specs = (
        P("shot", "slab", None, None),
        P("shot", "slab", None, None),
        P("slab", None, None),
        P("shot", None, None),
        P("shot", None),
        P("shot"),
        P("shot", None, None),
    )
    out_specs = (P("slab", "shot", None), P("shot", "slab", None, None))
    return jax.shard_map(
        on_device, mesh=mesh, in_specs=in_specs, out_specs=out_specs, check_vma=False
    )
```

profile of v0, /device:TPU:12, one launch (start us, length us, event | category | flops | bytes accessed | tf_op | source)
XLA Modules:
  0.0 1976.4 jit_solution(910315891626935429)
XLA Ops:
  13.4 1935.7 %while.62 = (s32[]{:T(128)}, f32[2,16,64,128]{3,2,1,0:T(8,128)}, f32[2,16,64,128]{3,2,1,0:T(8,128)S(1)}, f32[16,64,128]{2,1,0:T(8,128)}, s32[1,2048]{1,0:T(1,128...) while((s32[]{:T(128)}, f32[2,16,64,128]{3,2,1,0:T(8,128)}, ...), condition=%wide.region_4.5_spmd.clone, body=%wide.region_0.4_spmd.clone.sunk | while | flops 12513304 | bytes 62303260 | solution.py:108
  15.2 31.1 %broadcast.247 = f32[196608,8]{1,0:T(8,128)} broadcast(f32[]{:T(128)} %constant.235.clone.1..sunk), dimensions={} | broadcast | bytes 6291460 | tf_op jit(solution)/shard_map/while
  46.3 261.7 %scatter_fusion = f32[196608,8]{1,0:T(8,128)} fusion(f32[196608,8]{1,0:T(8,128)} %broadcast.247, s32[2048]{0:T(1024)S(1)} %broadcast_select_fusion.2, f32[2048,8]{1,0:T(8,128)S(1)} %select_bitcast_fusion.2), kind=kCustom, calls=%fused_computation.clone.clone.1 | custom fusion | flops 16384 | bytes 204800 | tf_op jit(solution)/shard_map/while
  308.0 50.7 %copy.17 = f32[1,8,196608]{2,1,0:T(8,128)} copy(f32[1,8,196608]{1,2,0:T(8,128)} %bitcast.30) | data formatting | bytes 12582912 | tf_op jit(solution)/shard_map/while/body/eval_jaxpr/while | solution.py:102
  358.7 137.0 %while.63 = (s32[]{:T(128)}, f32[2,16,64,128]{3,2,1,0:T(8,128)}, f32[2,16,64,128]{3,2,1,0:T(8,128)S(1)}, f32[16,64,128]{2,1,0:T(8,128)}, s32[]{:T(128)}, /*index...) while((s32[]{:T(128)}, f32[2,16,64,128]{3,2,1,0:T(8,128)}, ...), condition=%wide.region_3.3_spmd, body=%wide.region_2.2_spmd.sunk | while | flops 12451856 | bytes 41976360 | solution.py:102
  376.0 4.0 collective-permute-start
  393.2 4.0 collective-permute-start
  410.5 4.0 collective-permute-start
  427.7 4.0 collective-permute-start
  444.9 4.0 collective-permute-start
  462.1 4.0 collective-permute-start
  479.4 4.0 collective-permute-start
  497.6 31.1 %broadcast.247 = f32[196608,8]{1,0:T(8,128)} broadcast(f32[]{:T(128)} %constant.235.clone.1..sunk), dimensions={} | broadcast | bytes 6291460 | tf_op jit(solution)/shard_map/while
  528.7 261.7 %scatter_fusion = f32[196608,8]{1,0:T(8,128)} fusion(f32[196608,8]{1,0:T(8,128)} %broadcast.247, s32[2048]{0:T(1024)S(1)} %broadcast_select_fusion.2, f32[2048,8]{1,0:T(8,128)S(1)} %select_bitcast_fusion.2), kind=kCustom, calls=%fused_computation.clone.clone.1 | custom fusion | flops 16384 | bytes 204800 | tf_op jit(solution)/shard_map/while
  790.4 50.7 %copy.17 = f32[1,8,196608]{2,1,0:T(8,128)} copy(f32[1,8,196608]{1,2,0:T(8,128)} %bitcast.30) | data formatting | bytes 12582912 | tf_op jit(solution)/shard_map/while/body/eval_jaxpr/while | solution.py:102
  841.1 139.1 %while.63 = (s32[]{:T(128)}, f32[2,16,64,128]{3,2,1,0:T(8,128)}, f32[2,16,64,128]{3,2,1,0:T(8,128)S(1)}, f32[16,64,128]{2,1,0:T(8,128)}, s32[]{:T(128)}, /*index...) while((s32[]{:T(128)}, f32[2,16,64,128]{3,2,1,0:T(8,128)}, ...), condition=%wide.region_3.3_spmd, body=%wide.region_2.2_spmd.sunk | while | flops 12451856 | bytes 41976360 | solution.py:102
  842.0 4.8 collective-permute-start
  860.5 3.2 collective-permute-start
  877.7 3.2 collective-permute-start
  894.9 3.2 collective-permute-start
  912.1 3.2 collective-permute-start
  929.4 3.2 collective-permute-start
  946.6 3.2 collective-permute-start
  963.8 3.2 collective-permute-start
  982.0 31.1 %broadcast.247 = f32[196608,8]{1,0:T(8,128)} broadcast(f32[]{:T(128)} %constant.235.clone.1..sunk), dimensions={} | broadcast | bytes 6291460 | tf_op jit(solution)/shard_map/while
  1013.1 261.7 %scatter_fusion = f32[196608,8]{1,0:T(8,128)} fusion(f32[196608,8]{1,0:T(8,128)} %broadcast.247, s32[2048]{0:T(1024)S(1)} %broadcast_select_fusion.2, f32[2048,8]{1,0:T(8,128)S(1)} %select_bitcast_fusion.2), kind=kCustom, calls=%fused_computation.clone.clone.1 | custom fusion | flops 16384 | bytes 204800 | tf_op jit(solution)/shard_map/while
  1274.8 50.7 %copy.17 = f32[1,8,196608]{2,1,0:T(8,128)} copy(f32[1,8,196608]{1,2,0:T(8,128)} %bitcast.30) | data formatting | bytes 12582912 | tf_op jit(solution)/shard_map/while/body/eval_jaxpr/while | solution.py:102
  1325.6 139.1 %while.63 = (s32[]{:T(128)}, f32[2,16,64,128]{3,2,1,0:T(8,128)}, f32[2,16,64,128]{3,2,1,0:T(8,128)S(1)}, f32[16,64,128]{2,1,0:T(8,128)}, s32[]{:T(128)}, /*index...) while((s32[]{:T(128)}, f32[2,16,64,128]{3,2,1,0:T(8,128)}, ...), condition=%wide.region_3.3_spmd, body=%wide.region_2.2_spmd.sunk | while | flops 12451856 | bytes 41976360 | solution.py:102
  1326.4 4.0 collective-permute-start
  1347.3 3.3 collective-permute-start.1
  1364.5 3.3 collective-permute-start.1
  1381.8 3.3 collective-permute-start.1
  1399.0 3.3 collective-permute-start.1
  1416.2 3.3 collective-permute-start.1
  1433.4 3.3 collective-permute-start.1
  1450.6 3.3 collective-permute-start.1
  1466.5 31.1 %broadcast.247 = f32[196608,8]{1,0:T(8,128)} broadcast(f32[]{:T(128)} %constant.235.clone.1..sunk), dimensions={} | broadcast | bytes 6291460 | tf_op jit(solution)/shard_map/while
  1497.6 261.7 %scatter_fusion = f32[196608,8]{1,0:T(8,128)} fusion(f32[196608,8]{1,0:T(8,128)} %broadcast.247, s32[2048]{0:T(1024)S(1)} %broadcast_select_fusion.2, f32[2048,8]{1,0:T(8,128)S(1)} %select_bitcast_fusion.2), kind=kCustom, calls=%fused_computation.clone.clone.1 | custom fusion | flops 16384 | bytes 204800 | tf_op jit(solution)/shard_map/while
  1759.2 50.7 %copy.17 = f32[1,8,196608]{2,1,0:T(8,128)} copy(f32[1,8,196608]{1,2,0:T(8,128)} %bitcast.30) | data formatting | bytes 12582912 | tf_op jit(solution)/shard_map/while/body/eval_jaxpr/while | solution.py:102
  1810.0 139.1 %while.63 = (s32[]{:T(128)}, f32[2,16,64,128]{3,2,1,0:T(8,128)}, f32[2,16,64,128]{3,2,1,0:T(8,128)S(1)}, f32[16,64,128]{2,1,0:T(8,128)}, s32[]{:T(128)}, /*index...) while((s32[]{:T(128)}, f32[2,16,64,128]{3,2,1,0:T(8,128)}, ...), condition=%wide.region_3.3_spmd, body=%wide.region_2.2_spmd.sunk | while | flops 12451856 | bytes 41976360 | solution.py:102
  1831.3 3.8 collective-permute-start.1
  1848.5 3.8 collective-permute-start.1
  1865.7 3.8 collective-permute-start.1
  1882.9 3.8 collective-permute-start.1
  1900.2 3.8 collective-permute-start.1
  1917.4 3.8 collective-permute-start.1
  1934.6 3.8 collective-permute-start.1
  1950.0 17.8 reduce-scatter.2.cloned.1.call-done
  (733 shorter events, 453.2 us)
Async XLA Ops:
  7.2 1960.6 %reduce-scatter.2.cloned.1.call-start = ((), (), s32[]{:S(2)}) async-start(), calls=%async_computation.1 | async-start | bytes 786432 | tf_op jit(solution)/shard_map/reduce_scatter | solution.py:111
  359.6 8.9 collective-permute-start
  376.0 9.2 collective-permute-start
  393.2 9.2 collective-permute-start
  410.5 9.2 collective-permute-start
  427.7 9.2 collective-permute-start
  444.9 9.2 collective-permute-start
  462.1 9.2 collective-permute-start
  479.4 9.2 collective-permute-start
  842.0 10.0 collective-permute-start
  860.5 9.0 collective-permute-start
  877.7 9.0 collective-permute-start
  894.9 9.0 collective-permute-start
  912.1 9.0 collective-permute-start
  929.4 9.0 collective-permute-start
  946.6 9.0 collective-permute-start
  963.8 9.0 collective-permute-start
  1326.4 9.2 collective-permute-start
  1344.9 9.0 collective-permute-start
  1347.3 8.8 collective-permute-start.1
  1362.1 9.0 collective-permute-start
  1364.5 8.8 collective-permute-start.1
  1379.4 9.0 collective-permute-start
  1381.8 8.8 collective-permute-start.1
  1396.6 9.0 collective-permute-start
  1399.0 8.8 collective-permute-start.1
  1413.8 9.0 collective-permute-start
  1416.2 8.8 collective-permute-start.1
  1431.0 9.0 collective-permute-start
  1433.4 8.8 collective-permute-start.1
  1448.2 9.0 collective-permute-start
  1450.6 8.8 collective-permute-start.1
  1810.8 8.9 collective-permute-start
  1814.0 9.2 collective-permute-start.1
  1829.3 9.0 collective-permute-start
  1831.3 9.2 collective-permute-start.1
  1846.6 9.0 collective-permute-start
  1848.5 9.2 collective-permute-start.1
  1863.8 9.0 collective-permute-start
  1865.7 9.2 collective-permute-start.1
  1881.0 9.0 collective-permute-start
  1882.9 9.2 collective-permute-start.1
  1898.2 9.0 collective-permute-start
  1900.2 9.2 collective-permute-start.1
  1915.5 9.0 collective-permute-start
  1917.4 9.2 collective-permute-start.1
  1932.7 9.0 collective-permute-start
  1934.6 9.2 collective-permute-start.1
  (151 other events, 420.1 us)
Sparse Core Ops, SparseCore 0:
  1949.2 18.5 reduce-scatter.1
where the time goes:
time: 2010 us; the launch traced here: 1980 us
  other arithmetic  1150 us (57%)
  local copies, waits for them, and re-layouts  569 us (28%)
  starting transfers between devices  186 us (9%)
  waiting for transfers between devices  46.6 us (2%)
    while x16, other arithmetic  1050 us
    while x4, local copies, waits for them, and re-layouts, block_run(): lax.fori_loop(BLOCK_STEPS * b, BLOCK_STEPS * b + BLOCK_STEPS, one_step, c...  203 us
    while x388, local copies, waits for them, and re-layouts  200 us
    dynamic_slice x32, local copies, waits for them, and re-layouts, sources(): l_part = lax.dynamic_index_in_dim(table, step - lowest, 1, keepdims=False)  101 us
    ppermute x32, starting transfers between devices, with_halo(): before = lax.ppermute(last, axis, up)  95.2 us
    ppermute x32, starting transfers between devices, with_halo(): after = lax.ppermute(initial, axis, down)  90.4 us
    add x32, other arithmetic, one_step(): fresh = 2.0 * cur - nxt + coef * (lap_now + sources(step, table, lowest))  86.6 us
  transfers between devices with their start and end apart: 65, of which 33 were waited for; matrix products, arithmetic and copies ran while one was open for 7% of the time, Pallas kernels for 0%

commit v1 on v0

v1 whole, which is shorter than its diff:
```python
import functools

import jax
import jax.numpy as jnp
from jax import lax
from jax.experimental import pallas as pl
from jax.experimental.pallas import tpu as pltpu
from jax.sharding import PartitionSpec as P

COEFS = (-205.0 / 72.0, 8.0 / 5.0, -1.0 / 5.0, 8.0 / 315.0, -1.0 / 560.0)
REACH = 4
SHIFT = 8
VMEM_BYTES = 40 * 1024 * 1024
SUB = 8

MSG = 2 * SHIFT + REACH
REST = SHIFT + REACH
SPAN = 32
MID = 12


def ricker(step):
    arg = (jnp.pi * 0.06 * (step - 10.0)) ** 2
    return 10.0 * (1.0 - 2.0 * arg) * jnp.exp(-arg)


def tiled(field):
    layers, width_x, width_y = field.shape
    return field.reshape(layers, SUB, width_x // SUB, width_y).transpose(0, 2, 1, 3)


def untiled(field):
    layers, parts, sub, width_y = field.shape
    return field.transpose(0, 2, 1, 3).reshape(layers, sub * parts, width_y)


def lap_maker(parts, width_y):
    lane = lax.broadcasted_iota(jnp.int32, (1, SUB, width_y), 2)
    row = lax.broadcasted_iota(jnp.int32, (1, SUB, width_y), 1)
    plus = [jnp.where(lane < width_y - k, COEFS[k], 0.0).astype(jnp.float32) for k in range(1, 5)]
    minus = [jnp.where(lane >= k, COEFS[k], 0.0).astype(jnp.float32) for k in range(1, 5)]

    def lap(ref, j):
        f = ref[j]
        after = jnp.where(row == SUB - 1, 0.0, pltpu.roll(f[:REACH], SUB - 1, 1))
        before = jnp.where(row == 0, 0.0, pltpu.roll(f[parts - REACH :], 1, 1))
        wide = jnp.concatenate([before, f, after], axis=0)
        total = (3.0 * COEFS[0]) * f
        for k in range(1, 5):
            pair = (ref[j + k] + ref[j - k]) + (
                wide[REACH + k : REACH + k + parts] + wide[REACH - k : REACH - k + parts]
            )
            total = total + COEFS[k] * pair
            total = total + plus[k - 1] * pltpu.roll(f, width_y - k, 2)
            total = total + minus[k - 1] * pltpu.roll(f, k, 2)
        return f, total

    return lap


def layers_loop(first, count, body):
    def one(q, carry):
        body(first + q)
        return carry

    lax.fori_loop(0, count, one, 0, unroll=2)


def inject(rbuf, rl, ids, starts, res, level, first, last, bits, width_y):
    lane = lax.broadcasted_iota(jnp.int32, (1, width_y), 1)

    def one(r, carry):
        place = rl[r]
        who = ids[r]
        row = lax.shift_right_logical(place, bits)
        col = place & ((1 << bits) - 1)
        value = res[level, lax.shift_right_logical(who, 7), who & 127]
        spot = rbuf[pl.ds(row, 1), :]
        rbuf[pl.ds(row, 1), :] = spot + jnp.where(lane == col, value, 0.0)
        return carry

    lax.fori_loop(starts[first], starts[last], one, 0)


def block_kernel(side, is_l, bits, *refs):
    refs = list(refs)

    def take(count):
        got = refs[:count]
        del refs[:count]
        return got

    (scal,) = take(1)
    wave = rl = ids = starts = res_hbm = x_in = g_in = vmsg_in = None
    if is_l:
        rl, ids, starts, res_hbm = take(4)
    else:
        (wave,) = take(1)
    own, rest, recv, coef = take(4)
    if side == 1:
        (vmsg_in,) = take(1)
    if is_l:
        x_in, g_in = take(2)
    msg_out, rest_out = take(2)
    vmsg_out = x_out = g = None
    if side == 0:
        (vmsg_out,) = take(1)
    if is_l:
        (g,) = take(1)
    else:
        (x_out,) = take(1)
    a, b, c, p = take(4)
    rbuf = res = sem = None
    if is_l:
        rbuf, res, sem = take(3)

    parts, _, width_y = a.shape[1:]
    rows = parts * SUB
    n0, is_last, src_layer, src_part, src_row, src_lane = (scal[i] for i in range(6))
    off = MID - SHIFT if side == 0 else MID - 2 * SHIFT
    lap = lap_maker(parts, width_y)

    if is_l:
        fetch = pltpu.make_async_copy(res_hbm.at[pl.ds(n0 - 1, 3)], res, sem)
        fetch.start()
        rbuf[...] = jnp.zeros(rbuf.shape, jnp.float32)

    def bring(msg, low):
        if low:
            a[MID - SHIFT : MID] = msg[0:SHIFT]
            p[MID - REACH : MID] = msg[SHIFT : SHIFT + REACH]
            b[MID - SHIFT - REACH : MID - REACH] = msg[SHIFT + REACH : MSG]
        else:
            a[MID : MID + SHIFT] = msg[0:SHIFT]
            p[MID : MID + REACH] = msg[SHIFT : SHIFT + REACH]
            b[MID + REACH : MID + REACH + SHIFT] = msg[SHIFT + REACH : MSG]

    if side == 0:
        bring(recv, True)
        a[MID : MID + SHIFT] = rest[0:SHIFT]
        p[MID : MID + REACH] = rest[SHIFT:REST]
        b[MID + REACH : MID + REACH + SHIFT] = own[SHIFT + REACH : MSG]

        @pl.when(is_last == 1)
        def _():
            zero = jnp.zeros((REACH,) + a.shape[1:], jnp.float32)
            a[MID + SHIFT : MID + 2 * SHIFT] = own[0:SHIFT]
            p[MID + SHIFT + REACH : MID + 2 * SHIFT] = own[SHIFT : SHIFT + REACH]
            for field in (a, b, c):
                field[MID + 2 * SHIFT : MID + 2 * SHIFT + REACH] = zero
    else:
        a[MID - SHIFT : MID] = rest[0:SHIFT]
        p[MID - REACH : MID] = rest[SHIFT:REST]
        b[MID - SHIFT - REACH : MID - REACH] = own[SHIFT + REACH : MSG]

        @pl.when(is_last == 1)
        def _():
            bring(vmsg_in, False)

        @pl.when(is_last == 0)
        def _():
            bring(recv, False)

    if is_l:
        fetch.wait()

    def source(nxt, level, first, count):
        j = src_layer + off

        @pl.when((src_layer >= 0) & (j >= first) & (j < first + count))
        def _():
            lane = lax.broadcasted_iota(jnp.int32, (1, width_y), 1)
            spot = nxt[j, src_part, pl.ds(src_row, 1), :]
            gain = coef[src_layer, src_part, pl.ds(src_row, 1), :] * wave[n0 + 1 - level]
            nxt[j, src_part, pl.ds(src_row, 1), :] = spot - jnp.where(lane == src_lane, gain, 0.0)

    def advance(level, cur, nxt, first, count, x_base, outs, x_save=None):
        if is_l:
            zone = (first - off) // REACH
            inject(rbuf, rl, ids, starts, res, 2 - level, zone, zone + count // REACH, bits, width_y)
        else:
            source(nxt, level, first, count)

        def body(j):
            f, total = lap(cur, j)
            if is_l:
                at = pl.multiple_of((j - off) * rows, rows)
                total = total + rbuf[pl.ds(at, rows), :].reshape(parts, SUB, width_y)
                rbuf[pl.ds(at, rows), :] = jnp.zeros((rows, width_y), jnp.float32)
            step = coef[j - off] * total
            new = (2.0 * f - nxt[j]) + step
            for ref, shift in outs:
                ref[j + shift] = new
            if is_l:
                g[j - off] = g[j - off] + x_in[j + (x_base - first)] * step
            else:
                x_out[j + (x_base - first)] = f

        layers_loop(first, count, body)

    if is_l:
        if side == 0:
            g[2 * SHIFT : 3 * SHIFT] = g_in[2 * SHIFT : 3 * SHIFT]
            g[0 : 2 * SHIFT] = g_in[0 : 2 * SHIFT]
        else:
            g[...] = g_in[...]

    advance(0, a, p, MID - REACH, SHIFT, 0, [(b, 0)])
    if side == 0:

        @pl.when(is_last == 1)
        def _():
            advance(0, a, p, MID + SHIFT + REACH, REACH, 32, [(b, 0)])

    advance(1, b, a, MID - SHIFT, 2 * SHIFT, 8, [(c, 0)])
    if side == 0:

        @pl.when(is_last == 1)
        def _():
            advance(1, b, a, MID + SHIFT, SHIFT, 36, [(c, 0)])
            vmsg_out[0:SHIFT] = c[MID + SHIFT : MID + 2 * SHIFT]
            vmsg_out[SHIFT : SHIFT + REACH] = b[MID + SHIFT : MID + SHIFT + REACH]
            vmsg_out[SHIFT + 2 * REACH : MSG] = jnp.zeros((REACH,) + a.shape[1:], jnp.float32)

    if side == 0:
        msg_out[0:SHIFT] = c[MID - SHIFT : MID]
        msg_out[SHIFT : SHIFT + REACH] = b[MID - SHIFT : MID - REACH]
        rest_out[0:SHIFT] = c[MID : MID + SHIFT]
        rest_out[SHIFT:REST] = b[MID + REACH : MID + SHIFT]
    else:
        msg_out[0:SHIFT] = c[MID : MID + SHIFT]
        msg_out[SHIFT : SHIFT + REACH] = b[MID + REACH : MID + SHIFT]
        rest_out[0:SHIFT] = c[MID - SHIFT : MID]
        rest_out[SHIFT:REST] = b[MID - SHIFT : MID - REACH]

    @pl.when(n0 >= 2)
    def _():
        advance(2, c, b, MID - REACH, SHIFT, 24, [(msg_out, SHIFT + REACH - (MID - REACH))])
        if side == 0:

            @pl.when(is_last == 1)
            def _():
                first = MID + SHIFT + REACH
                advance(2, c, b, first, REACH, 44, [(vmsg_out, SHIFT + REACH - first)])

    @pl.when(n0 < 2)
    def _():
        msg_out[SHIFT + REACH : MSG] = jnp.zeros((SHIFT,) + a.shape[1:], jnp.float32)


def first_u_kernel(scal, wave, f0, f1, coef, msg_out, rest_out):
    depth, parts, _, width_y = f0.shape
    n0, _, src_layer, src_part, src_row, src_lane = (scal[i] for i in range(6))
    lap = lap_maker(parts, width_y)
    msg_out[0:SHIFT] = f0[depth - SHIFT : depth]
    msg_out[SHIFT : SHIFT + REACH] = f1[depth - REACH : depth]
    rest_out[0:SHIFT] = f0[0:SHIFT]
    rest_out[SHIFT:REST] = f1[0:REACH]

    def body(j):
        f, total = lap(f0, j)
        msg_out[j + SHIFT] = (2.0 * f - f1[j]) + coef[j] * total

    layers_loop(REACH, SHIFT, body)
    j = src_layer - SHIFT

    @pl.when((src_layer >= 0) & (j >= REACH) & (j < REACH + SHIFT))
    def _():
        lane = lax.broadcasted_iota(jnp.int32, (1, width_y), 1)
        spot = msg_out[j + SHIFT, src_part, pl.ds(src_row, 1), :]
        gain = coef[j, src_part, pl.ds(src_row, 1), :] * wave[n0 + 1]
        msg_out[j + SHIFT, src_part, pl.ds(src_row, 1), :] = spot + jnp.where(lane == src_lane, gain, 0.0)


def first_l_kernel(bits, scal, rl, ids, starts, res_hbm, f0, coef, msg_out, rest_out, g, rbuf, res, sem):
    depth, parts, _, width_y = f0.shape
    rows = parts * SUB
    fetch = pltpu.make_async_copy(res_hbm.at[pl.ds(scal[0] - 1, 3)], res, sem)
    fetch.start()
    rbuf[...] = jnp.zeros(rbuf.shape, jnp.float32)
    msg_out[0 : SHIFT + REACH] = jnp.zeros((SHIFT + REACH,) + f0.shape[1:], jnp.float32)
    rest_out[...] = jnp.zeros(rest_out.shape, jnp.float32)
    g[...] = jnp.zeros(g.shape, jnp.float32)
    fetch.wait()
    zone = (SHIFT + REACH) // REACH
    inject(rbuf, rl, ids, starts, res, 2, zone, zone + SHIFT // REACH, bits, width_y)

    def body(j):
        at = pl.multiple_of((j + SHIFT) * rows, rows)
        new = coef[j] * rbuf[pl.ds(at, rows), :].reshape(parts, SUB, width_y)
        msg_out[j + SHIFT] = new
        g[j + SHIFT] = f0[j] * new

    layers_loop(REACH, SHIFT, body)


def on_device(fwd_last, fwd_prev, velocity, aperture, rec_index, src_index, residual):
    _, depth, width_x, width_y = fwd_last.shape
    parts = width_x // SUB
    total_steps, receivers = residual.shape[1:]
    plane = width_x * width_y
    slabs = lax.axis_size("slab")
    slab = lax.axis_index("slab")
    up = [(i, i + 1) for i in range(slabs - 1)]
    down = [(i + 1, i) for i in range(slabs - 1)]
    bits = (width_y - 1).bit_length()
    f32 = jnp.float32

    vel_left = lax.ppermute(velocity[depth - SHIFT :], "slab", up)
    coef_own = tiled((0.4 * velocity) ** 2)
    coef = jnp.concatenate([tiled((0.4 * vel_left) ** 2), coef_own], axis=0)

    base = (slab * depth - SHIFT) * plane
    window = (depth + SHIFT) * plane
    local = rec_index[0] - base
    far = jnp.int32(2**30)
    keys = jnp.where((local >= 0) & (local < window), local, far)
    keys, ids = lax.sort((keys, lax.iota(jnp.int32, receivers)), num_keys=1, is_stable=False)

    def place_of(cell):
        layer = cell // plane
        x = (cell // width_y) % width_x
        return layer, x % parts, x // parts, cell % width_y

    layer, part, row, lane = place_of(keys)
    rl = (((layer * parts + part) * SUB + row) << bits) | lane
    zones = (depth + SHIFT) // REACH
    edges = jnp.arange(zones + 1, dtype=jnp.int32) * (REACH * plane)
    starts = jnp.sum((keys[None, :] < edges[:, None]).astype(jnp.int32), axis=1)

    src = src_index[0] - base
    src_in = (src >= 0) & (src < window)
    s_layer, s_part, s_row, s_lane = place_of(jnp.where(src_in, src, 0))
    s_layer = jnp.where(src_in, s_layer, -1)
    is_last = (slab == slabs - 1).astype(jnp.int32)

    def scal_of(n0):
        return jnp.stack([jnp.asarray(n0, jnp.int32), is_last, s_layer, s_part, s_row, s_lane])

    wave = jnp.concatenate([jnp.zeros((1,), f32), ricker(jnp.arange(total_steps, dtype=f32))])
    res = jnp.concatenate([jnp.zeros((1, receivers), f32), residual[0]]).reshape(
        total_steps + 1, receivers // 128, 128
    )

    smem = pl.BlockSpec(memory_space=pltpu.SMEM)
    vmem = pl.BlockSpec(memory_space=pltpu.VMEM)
    anym = pl.BlockSpec(memory_space=pl.ANY)

    def fields(layers):
        return jax.ShapeDtypeStruct((layers, parts, SUB, width_y), f32)

    params = pltpu.CompilerParams(vmem_limit_bytes=VMEM_BYTES)
    l_scratch = [
        pltpu.VMEM(((depth + SHIFT) * parts * SUB, width_y), f32),
        pltpu.SMEM((3, receivers // 128, 128), f32),
        pltpu.SemaphoreType.DMA(()),
    ]
    layer_bytes = 4 * plane

    def cost(layers):
        return pl.CostEstimate(
            flops=50 * layers * plane, bytes_accessed=6 * layers * layer_bytes, transcendentals=0
        )

    f0, f1 = tiled(fwd_prev[0]), tiled(fwd_last[0])
    um, ur = pl.pallas_call(
        first_u_kernel,
        out_shape=(fields(MSG), fields(REST)),
        in_specs=[smem, smem, vmem, vmem, vmem],
        out_specs=(vmem, vmem),
        compiler_params=params,
        cost_estimate=cost(SHIFT),
        name="first_u",
    )(scal_of(total_steps - 1), wave, f0, f1, coef_own)
    lm, lr, g = pl.pallas_call(
        functools.partial(first_l_kernel, bits),
        out_shape=(fields(MSG), fields(REST), fields(depth + SHIFT)),
        in_specs=[smem, smem, smem, smem, anym, vmem, vmem],
        out_specs=(vmem, vmem, vmem),
        scratch_shapes=l_scratch,
        compiler_params=params,
        cost_estimate=cost(SHIFT),
        name="first_l",
    )(scal_of(total_steps - 1), rl, ids, starts, res, f0, coef_own)

    def u_block(side, n0, own, rest, recv, *vmsg):
        outs = [fields(MSG), fields(REST)]
        if side == 0:
            outs.append(fields(MSG))
        outs.append(fields(48))
        return pl.pallas_call(
            functools.partial(block_kernel, side, False, bits),
            out_shape=outs,
            in_specs=[smem, smem] + [vmem] * (4 + len(vmsg)),
            out_specs=[vmem] * len(outs),
            scratch_shapes=[pltpu.VMEM((SPAN, parts, SUB, width_y), f32)] * 4,
            compiler_params=params,
            cost_estimate=cost(2 * depth),
            name=f"u_block{side}",
        )(scal_of(n0), wave, own, rest, recv, coef, *vmsg)

    def l_block(side, n0, own, rest, recv, vmsg, x, g):
        outs = [fields(MSG), fields(REST)]
        if side == 0:
            outs.append(fields(MSG))
        outs.append(fields(depth + SHIFT))
        return pl.pallas_call(
            functools.partial(block_kernel, side, True, bits),
            out_shape=outs,
            in_specs=[smem] * 4 + [anym] + [vmem] * (6 + len(vmsg)),
            out_specs=[vmem] * len(outs),
            scratch_shapes=[pltpu.VMEM((SPAN, parts, SUB, width_y), f32)] * 4 + l_scratch,
            compiler_params=params,
            cost_estimate=cost(2 * depth),
            name=f"l_block{side}",
        )(scal_of(n0), rl, ids, starts, res, own, rest, recv, coef, *vmsg, x, g)

    def two_blocks(i, carry):
        um, ur, u_got, lm, lr, g = carry
        n0 = total_steps - 1 - 4 * i
        l_got = lax.ppermute(lm, "slab", up)
        um, ur, uv, x = u_block(0, n0, um, ur, u_got)
        u_got = lax.ppermute(um, "slab", down)
        lm, lr, lv, g = l_block(0, n0, lm, lr, l_got, (), x, g)
        l_got = lax.ppermute(lm, "slab", down)
        um, ur, x = u_block(1, n0 - 2, um, ur, u_got, uv)
        u_got = lax.ppermute(um, "slab", up)
        lm, lr, g = l_block(1, n0 - 2, lm, lr, l_got, (lv,), x, g)
        return (um, ur, u_got, lm, lr, g)

    u_got = lax.ppermute(um, "slab", up)
    um, ur, u_got, lm, lr, g = lax.fori_loop(0, total_steps // 4, two_blocks, (um, ur, u_got, lm, lr, g))

    adjoint_field = untiled(jnp.concatenate([lr[:SHIFT], lm[:SHIFT]], axis=0))[None]
    g_right = lax.ppermute(g[:SHIFT], "slab", down)
    g = jnp.concatenate([g[SHIFT : 2 * SHIFT], g[2 * SHIFT :] + g_right], axis=0)
    g = aperture[0].astype(f32) * untiled(g)
    summed = lax.psum_scatter(g, "shot", scatter_dimension=1, tiled=True)
    block = width_x // lax.axis_size("shot")
    speed = lax.dynamic_slice_in_dim(velocity, lax.axis_index("shot") * block, block, 1)
    return ((-2.0 / speed) * summed, adjoint_field)


def solution(mesh):
    in_specs = (
        P("shot", "slab", None, None),
        P("shot", "slab", None, None),
        P("slab", None, None),
        P("shot", None, None),
        P("shot", None),
        P("shot"),
        P("shot", None, None),
    )
    out_specs = (P("slab", "shot", None), P("shot", "slab", None, None))
    return jax.shard_map(on_device, mesh=mesh, in_specs=in_specs, out_specs=out_specs, check_vma=False)
```

time: 2010 us -> 481 us (0.24); the launches traced: 1980 us -> 473 us
  other arithmetic: 1150 us -> 10.3 us
  local copies, waits for them, and re-layouts: 569 us -> 49 us
  Pallas kernels: 0 us -> 250 us
  starting transfers between devices: 186 us -> 111 us
    while x16 -> x0, other arithmetic: 1050 us -> none
    while x392 -> x128, local copies, waits for them, and re-layouts: 402 us -> 43.3 us  [the longest x4 203 us: block_run(): lax.fori_loop(BLOCK_STEPS * b, BLOCK_STEPS * b + BLOCK_STEPS, one_step, c...]
    pallas_call x0 -> x34, Pallas kernels: none -> 250 us  [the longest x16 147 us: l_block(): pl.pallas_call(functools.partial(block_kernel, side, True, bits), out_sha...]
    dynamic_slice x40 -> x0, local copies, waits for them, and re-layouts: 105 us -> none  [the longest x32 101 us: sources(): l_part = lax.dynamic_index_in_dim(table, step - lowest, 1, keepdims=False)]
    add x64 -> x1, other arithmetic: 97.9 us -> 0.99 us  [on_device(): g = jnp.concatenate([g[SHIFT:2 * SHIFT], g[2 * SHIFT:] + g_right], axis=0)]
    ppermute x64 -> x35, starting transfers between devices: 186 us -> 111 us  [the longest x8 40.4 us: two_blocks(): l_got = lax.ppermute(lm, 'slab', up)]
    concatenate x34 -> x1, local copies, waits for them, and re-layouts: 33.3 us -> 0.03 us  [on_device(): jnp.concatenate([jnp.zeros((1, receivers), f32), residual[0]])]
    slice x33 -> x4, local copies, waits for them, and re-layouts: 27.3 us -> 2.12 us  [the longest x1 1.07 us: on_device(): g = jnp.concatenate([g[SHIFT:2 * SHIFT], g[2 * SHIFT:] + g_right], axis=0)]
  transfers between devices with their start and end apart: 65 -> 36, of which waited for: 33 -> 4; matrix products, arithmetic and copies ran while one was open for 7% -> 2% of each run, Pallas kernels for 0% -> 52%
where the time goes in v1:
time: 481 us; the launch traced here: 473 us
  Pallas kernels  250 us (52%)
  starting transfers between devices  111 us (23%)
  local copies, waits for them, and re-layouts  49 us (10%)
  waiting for transfers between devices  35.8 us (7%)
  between operations  15.2 us (3%)
  other arithmetic  10.3 us (2%)
    pallas_call x16, Pallas kernels, l_block(): pl.pallas_call(functools.partial(block_kernel, side, True, bits), out_sha...  147 us
    pallas_call x16, Pallas kernels, u_block(): pl.pallas_call(functools.partial(block_kernel, side, False, bits), out_sh...  96.5 us
    while x128, local copies, waits for them, and re-layouts  43.3 us
    ppermute x8, starting transfers between devices, two_blocks(): l_got = lax.ppermute(lm, 'slab', up)  40.4 us
    ppermute x8, starting transfers between devices, two_blocks(): u_got = lax.ppermute(um, 'slab', up)  28.5 us
    reduce_scatter x1, waiting for transfers between devices, on_device(): summed = lax.psum_scatter(g, 'shot', scatter_dimension=1, tiled=True)  24.8 us
    ppermute x8, starting transfers between devices, two_blocks(): u_got = lax.ppermute(um, 'slab', down)  17 us
    ppermute x8, starting transfers between devices, two_blocks(): l_got = lax.ppermute(lm, 'slab', down)  15.6 us
  transfers between devices with their start and end apart: 36, of which 4 were waited for; matrix products, arithmetic and copies ran while one was open for 2% of the time, Pallas kernels for 52%

profile of v1, /device:TPU:12, one launch (start us, length us, event | category | flops | bytes accessed | tf_op | source)
XLA Modules:
  0.0 472.9 jit_solution(16780603931596075349)
XLA Ops:
  17.7 4.3 sort.15
  23.1 3.8 first_l.1
  28.1 398.2 %while.27 = (s32[]{:T(128)}, f32[20,8,8,128]{3,2,1,0:T(8,128)}, f32[12,8,8,128]{3,2,1,0:T(8,128)}, f32[20,8,8,128]{3,2,1,0:T(8,128)}, f32[20,8,8,128]{3,2,1,0:T(...) while((s32[]{:T(128)}, f32[20,8,8,128]{3,2,1,0:T(8,128)}, ...), condition=%wide.region_3.4_spmd, body=%wide.region_2.3_spmd.sunk | while | flops 52428804 | bytes 54526664 | solution.py:432
  30.2 6.1 %u_block0.11 = (f32[20,8,8,128]{3,2,1,0:T(8,128)}, f32[12,8,8,128]{3,2,1,0:T(8,128)S(1)}, f32[20,8,8,128]{3,2,1,0:T(8,128)S(1)}, f32[48,8,8,128]{3,2,1,0:T(8,128)S(1)}) custom-call(s32[6]{0:T(128)S(1)} %stack.149.refs_0_, f32[33]{0:T(128)S(1)} %get-tuple-element.825.refs_1_, f32[20,8,8,128]{3,2,1,0:T(8,128)} %get-tuple-element.792.refs_2_, ...), custom_call_target="tpu_custom_call" | custom-call | flops 13107200 | bytes 6291456 | tf_op jit(solution)/shard_map/while/body/eval_jaxpr/u_block0/pallas_call | solution.py:391
  37.9 3.6 collective-permute-start
  43.6 8.9 %l_block0.11 = (f32[20,8,8,128]{3,2,1,0:T(8,128)S(1)}, f32[12,8,8,128]{3,2,1,0:T(8,128)S(1)}, f32[20,8,8,128]{3,2,1,0:T(8,128)S(1)}, f32[24,8,8,128]{3,2,1,0:T(8,128)S(1)}) custom-call(s32[6]{0:T(128)S(1)} %stack.149.refs_0_, s32[2048]{0:T(1024)S(1)} %get-tuple-element.827.refs_1_, s32[2048]{0:T(1024)S(1)} %get-tuple-element.828.refs_2_, ...), custom_call_target="tpu_custom_call" | custom-call | flops 13107200 | bytes 6291456 | tf_op jit(solution)/shard_map/while/body/eval_jaxpr/l_block0/pallas_call | solution.py:407
  55.5 6.1 %u_block1.11 = (f32[20,8,8,128]{3,2,1,0:T(8,128)}, f32[12,8,8,128]{3,2,1,0:T(8,128)}, f32[48,8,8,128]{3,2,1,0:T(8,128)S(1)}) custom-call(s32[6]{0:T(128)S(1)} %stack.148.refs_0_, f32[33]{0:T(128)S(1)} %get-tuple-element.825.refs_1_, f32[20,8,8,128]{3,2,1,0:T(8,128)} %get-tuple-element.755.refs_2_, f32[12,8,8,128]{3,2,1,0:T(8,128)S(1)} %copy-done.7, ...), custom_call_target="tpu_custom_call" | custom-call | flops 13107200 | bytes 6291456 | tf_op jit(solution)/shard_map/while/body/eval_jaxpr/u_block1/pallas_call | solution.py:391
  65.6 9.7 %l_block1.11 = (f32[20,8,8,128]{3,2,1,0:T(8,128)}, f32[12,8,8,128]{3,2,1,0:T(8,128)}, f32[24,8,8,128]{3,2,1,0:T(8,128)}) custom-call(s32[6]{0:T(128)S(1)} %stack.148.refs_0_, s32[2048]{0:T(1024)S(1)} %get-tuple-element.827.refs_1_, s32[2048]{0:T(1024)S(1)} %get-tuple-element.828.refs_2_, s32[7]{0:T(128)S(1)} %get-tuple-element.829.refs_3_, ...), custom_call_target="tpu_custom_call" | custom-call | flops 13107200 | bytes 6291456 | tf_op jit(solution)/shard_map/while/body/eval_jaxpr/l_block1/pallas_call | solution.py:407
  75.3 5.0 %collective-permute-start.2 = (f32[20,8,8,128]{3,2,1,0:T(8,128)}, f32[20,8,8,128]{3,2,1,0:T(8,128)S(1)}, u32[]{:S(2)}, u32[]{:S(2)}) collective-permute-start(f32[20,8,8,128]{3,2,1,0:T(8,128)} %get-tuple-element.795.refs_5_), channel_id=1, source_target_pairs={{0,1},{1,2},{2,3},{3,4},{4,5},{5,6},{6,7},{7,8},{8,9},{9,10},{10,1... | collective-permute-start | bytes 1966088 | tf_op jit(solution)/shard_map/while/body/eval_jaxpr/ppermute | solution.py:421
  80.5 6.1 %u_block0.11 = (f32[20,8,8,128]{3,2,1,0:T(8,128)}, f32[12,8,8,128]{3,2,1,0:T(8,128)S(1)}, f32[20,8,8,128]{3,2,1,0:T(8,128)S(1)}, f32[48,8,8,128]{3,2,1,0:T(8,128)S(1)}) custom-call(s32[6]{0:T(128)S(1)} %stack.149.refs_0_, f32[33]{0:T(128)S(1)} %get-tuple-element.825.refs_1_, f32[20,8,8,128]{3,2,1,0:T(8,128)} %get-tuple-element.792.refs_2_, ...), custom_call_target="tpu_custom_call" | custom-call | flops 13107200 | bytes 6291456 | tf_op jit(solution)/shard_map/while/body/eval_jaxpr/u_block0/pallas_call | solution.py:391
  92.1 8.9 %l_block0.11 = (f32[20,8,8,128]{3,2,1,0:T(8,128)S(1)}, f32[12,8,8,128]{3,2,1,0:T(8,128)S(1)}, f32[20,8,8,128]{3,2,1,0:T(8,128)S(1)}, f32[24,8,8,128]{3,2,1,0:T(8,128)S(1)}) custom-call(s32[6]{0:T(128)S(1)} %stack.149.refs_0_, s32[2048]{0:T(1024)S(1)} %get-tuple-element.827.refs_1_, s32[2048]{0:T(1024)S(1)} %get-tuple-element.828.refs_2_, ...), custom_call_target="tpu_custom_call" | custom-call | flops 13107200 | bytes 6291456 | tf_op jit(solution)/shard_map/while/body/eval_jaxpr/l_block0/pallas_call | solution.py:407
  103.7 6.1 %u_block1.11 = (f32[20,8,8,128]{3,2,1,0:T(8,128)}, f32[12,8,8,128]{3,2,1,0:T(8,128)}, f32[48,8,8,128]{3,2,1,0:T(8,128)S(1)}) custom-call(s32[6]{0:T(128)S(1)} %stack.148.refs_0_, f32[33]{0:T(128)S(1)} %get-tuple-element.825.refs_1_, f32[20,8,8,128]{3,2,1,0:T(8,128)} %get-tuple-element.755.refs_2_, f32[12,8,8,128]{3,2,1,0:T(8,128)S(1)} %copy-done.7, ...), custom_call_target="tpu_custom_call" | custom-call | flops 13107200 | bytes 6291456 | tf_op jit(solution)/shard_map/while/body/eval_jaxpr/u_block1/pallas_call | solution.py:391
  113.8 9.7 %l_block1.11 = (f32[20,8,8,128]{3,2,1,0:T(8,128)}, f32[12,8,8,128]{3,2,1,0:T(8,128)}, f32[24,8,8,128]{3,2,1,0:T(8,128)}) custom-call(s32[6]{0:T(128)S(1)} %stack.148.refs_0_, s32[2048]{0:T(1024)S(1)} %get-tuple-element.827.refs_1_, s32[2048]{0:T(1024)S(1)} %get-tuple-element.828.refs_2_, s32[7]{0:T(128)S(1)} %get-tuple-element.829.refs_3_, ...), custom_call_target="tpu_custom_call" | custom-call | flops 13107200 | bytes 6291456 | tf_op jit(solution)/shard_map/while/body/eval_jaxpr/l_block1/pallas_call | solution.py:407
  123.5 5.1 %collective-permute-start.2 = (f32[20,8,8,128]{3,2,1,0:T(8,128)}, f32[20,8,8,128]{3,2,1,0:T(8,128)S(1)}, u32[]{:S(2)}, u32[]{:S(2)}) collective-permute-start(f32[20,8,8,128]{3,2,1,0:T(8,128)} %get-tuple-element.795.refs_5_), channel_id=1, source_target_pairs={{0,1},{1,2},{2,3},{3,4},{4,5},{5,6},{6,7},{7,8},{8,9},{9,10},{10,1... | collective-permute-start | bytes 1966088 | tf_op jit(solution)/shard_map/while/body/eval_jaxpr/ppermute | solution.py:421
  128.7 6.1 %u_block0.11 = (f32[20,8,8,128]{3,2,1,0:T(8,128)}, f32[12,8,8,128]{3,2,1,0:T(8,128)S(1)}, f32[20,8,8,128]{3,2,1,0:T(8,128)S(1)}, f32[48,8,8,128]{3,2,1,0:T(8,128)S(1)}) custom-call(s32[6]{0:T(128)S(1)} %stack.149.refs_0_, f32[33]{0:T(128)S(1)} %get-tuple-element.825.refs_1_, f32[20,8,8,128]{3,2,1,0:T(8,128)} %get-tuple-element.792.refs_2_, ...), custom_call_target="tpu_custom_call" | custom-call | flops 13107200 | bytes 6291456 | tf_op jit(solution)/shard_map/while/body/eval_jaxpr/u_block0/pallas_call | solution.py:391
  140.3 8.9 %l_block0.11 = (f32[20,8,8,128]{3,2,1,0:T(8,128)S(1)}, f32[12,8,8,128]{3,2,1,0:T(8,128)S(1)}, f32[20,8,8,128]{3,2,1,0:T(8,128)S(1)}, f32[24,8,8,128]{3,2,1,0:T(8,128)S(1)}) custom-call(s32[6]{0:T(128)S(1)} %stack.149.refs_0_, s32[2048]{0:T(1024)S(1)} %get-tuple-element.827.refs_1_, s32[2048]{0:T(1024)S(1)} %get-tuple-element.828.refs_2_, ...), custom_call_target="tpu_custom_call" | custom-call | flops 13107200 | bytes 6291456 | tf_op jit(solution)/shard_map/while/body/eval_jaxpr/l_block0/pallas_call | solution.py:407
  152.0 6.1 %u_block1.11 = (f32[20,8,8,128]{3,2,1,0:T(8,128)}, f32[12,8,8,128]{3,2,1,0:T(8,128)}, f32[48,8,8,128]{3,2,1,0:T(8,128)S(1)}) custom-call(s32[6]{0:T(128)S(1)} %stack.148.refs_0_, f32[33]{0:T(128)S(1)} %get-tuple-element.825.refs_1_, f32[20,8,8,128]{3,2,1,0:T(8,128)} %get-tuple-element.755.refs_2_, f32[12,8,8,128]{3,2,1,0:T(8,128)S(1)} %copy-done.7, ...), custom_call_target="tpu_custom_call" | custom-call | flops 13107200 | bytes 6291456 | tf_op jit(solution)/shard_map/while/body/eval_jaxpr/u_block1/pallas_call | solution.py:391
  162.0 9.7 %l_block1.11 = (f32[20,8,8,128]{3,2,1,0:T(8,128)}, f32[12,8,8,128]{3,2,1,0:T(8,128)}, f32[24,8,8,128]{3,2,1,0:T(8,128)}) custom-call(s32[6]{0:T(128)S(1)} %stack.148.refs_0_, s32[2048]{0:T(1024)S(1)} %get-tuple-element.827.refs_1_, s32[2048]{0:T(1024)S(1)} %get-tuple-element.828.refs_2_, s32[7]{0:T(128)S(1)} %get-tuple-element.829.refs_3_, ...), custom_call_target="tpu_custom_call" | custom-call | flops 13107200 | bytes 6291456 | tf_op jit(solution)/shard_map/while/body/eval_jaxpr/l_block1/pallas_call | solution.py:407
  171.8 5.1 %collective-permute-start.2 = (f32[20,8,8,128]{3,2,1,0:T(8,128)}, f32[20,8,8,128]{3,2,1,0:T(8,128)S(1)}, u32[]{:S(2)}, u32[]{:S(2)}) collective-permute-start(f32[20,8,8,128]{3,2,1,0:T(8,128)} %get-tuple-element.795.refs_5_), channel_id=1, source_target_pairs={{0,1},{1,2},{2,3},{3,4},{4,5},{5,6},{6,7},{7,8},{8,9},{9,10},{10,1... | collective-permute-start | bytes 1966088 | tf_op jit(solution)/shard_map/while/body/eval_jaxpr/ppermute | solution.py:421
  177.0 6.1 %u_block0.11 = (f32[20,8,8,128]{3,2,1,0:T(8,128)}, f32[12,8,8,128]{3,2,1,0:T(8,128)S(1)}, f32[20,8,8,128]{3,2,1,0:T(8,128)S(1)}, f32[48,8,8,128]{3,2,1,0:T(8,128)S(1)}) custom-call(s32[6]{0:T(128)S(1)} %stack.149.refs_0_, f32[33]{0:T(128)S(1)} %get-tuple-element.825.refs_1_, f32[20,8,8,128]{3,2,1,0:T(8,128)} %get-tuple-element.792.refs_2_, ...), custom_call_target="tpu_custom_call" | custom-call | flops 13107200 | bytes 6291456 | tf_op jit(solution)/shard_map/while/body/eval_jaxpr/u_block0/pallas_call | solution.py:391
  188.6 8.9 %l_block0.11 = (f32[20,8,8,128]{3,2,1,0:T(8,128)S(1)}, f32[12,8,8,128]{3,2,1,0:T(8,128)S(1)}, f32[20,8,8,128]{3,2,1,0:T(8,128)S(1)}, f32[24,8,8,128]{3,2,1,0:T(8,128)S(1)}) custom-call(s32[6]{0:T(128)S(1)} %stack.149.refs_0_, s32[2048]{0:T(1024)S(1)} %get-tuple-element.827.refs_1_, s32[2048]{0:T(1024)S(1)} %get-tuple-element.828.refs_2_, ...), custom_call_target="tpu_custom_call" | custom-call | flops 13107200 | bytes 6291456 | tf_op jit(solution)/shard_map/while/body/eval_jaxpr/l_block0/pallas_call | solution.py:407
  200.2 6.1 %u_block1.11 = (f32[20,8,8,128]{3,2,1,0:T(8,128)}, f32[12,8,8,128]{3,2,1,0:T(8,128)}, f32[48,8,8,128]{3,2,1,0:T(8,128)S(1)}) custom-call(s32[6]{0:T(128)S(1)} %stack.148.refs_0_, f32[33]{0:T(128)S(1)} %get-tuple-element.825.refs_1_, f32[20,8,8,128]{3,2,1,0:T(8,128)} %get-tuple-element.755.refs_2_, f32[12,8,8,128]{3,2,1,0:T(8,128)S(1)} %copy-done.7, ...), custom_call_target="tpu_custom_call" | custom-call | flops 13107200 | bytes 6291456 | tf_op jit(solution)/shard_map/while/body/eval_jaxpr/u_block1/pallas_call | solution.py:391
  210.3 9.7 %l_block1.11 = (f32[20,8,8,128]{3,2,1,0:T(8,128)}, f32[12,8,8,128]{3,2,1,0:T(8,128)}, f32[24,8,8,128]{3,2,1,0:T(8,128)}) custom-call(s32[6]{0:T(128)S(1)} %stack.148.refs_0_, s32[2048]{0:T(1024)S(1)} %get-tuple-element.827.refs_1_, s32[2048]{0:T(1024)S(1)} %get-tuple-element.828.refs_2_, s32[7]{0:T(128)S(1)} %get-tuple-element.829.refs_3_, ...), custom_call_target="tpu_custom_call" | custom-call | flops 13107200 | bytes 6291456 | tf_op jit(solution)/shard_map/while/body/eval_jaxpr/l_block1/pallas_call | solution.py:407
  220.0 5.1 %collective-permute-start.2 = (f32[20,8,8,128]{3,2,1,0:T(8,128)}, f32[20,8,8,128]{3,2,1,0:T(8,128)S(1)}, u32[]{:S(2)}, u32[]{:S(2)}) collective-permute-start(f32[20,8,8,128]{3,2,1,0:T(8,128)} %get-tuple-element.795.refs_5_), channel_id=1, source_target_pairs={{0,1},{1,2},{2,3},{3,4},{4,5},{5,6},{6,7},{7,8},{8,9},{9,10},{10,1... | collective-permute-start | bytes 1966088 | tf_op jit(solution)/shard_map/while/body/eval_jaxpr/ppermute | solution.py:421
  225.2 6.1 %u_block0.11 = (f32[20,8,8,128]{3,2,1,0:T(8,128)}, f32[12,8,8,128]{3,2,1,0:T(8,128)S(1)}, f32[20,8,8,128]{3,2,1,0:T(8,128)S(1)}, f32[48,8,8,128]{3,2,1,0:T(8,128)S(1)}) custom-call(s32[6]{0:T(128)S(1)} %stack.149.refs_0_, f32[33]{0:T(128)S(1)} %get-tuple-element.825.refs_1_, f32[20,8,8,128]{3,2,1,0:T(8,128)} %get-tuple-element.792.refs_2_, ...), custom_call_target="tpu_custom_call" | custom-call | flops 13107200 | bytes 6291456 | tf_op jit(solution)/shard_map/while/body/eval_jaxpr/u_block0/pallas_call | solution.py:391
  236.8 8.9 %l_block0.11 = (f32[20,8,8,128]{3,2,1,0:T(8,128)S(1)}, f32[12,8,8,128]{3,2,1,0:T(8,128)S(1)}, f32[20,8,8,128]{3,2,1,0:T(8,128)S(1)}, f32[24,8,8,128]{3,2,1,0:T(8,128)S(1)}) custom-call(s32[6]{0:T(128)S(1)} %stack.149.refs_0_, s32[2048]{0:T(1024)S(1)} %get-tuple-element.827.refs_1_, s32[2048]{0:T(1024)S(1)} %get-tuple-element.828.refs_2_, ...), custom_call_target="tpu_custom_call" | custom-call | flops 13107200 | bytes 6291456 | tf_op jit(solution)/shard_map/while/body/eval_jaxpr/l_block0/pallas_call | solution.py:407
  248.5 6.1 %u_block1.11 = (f32[20,8,8,128]{3,2,1,0:T(8,128)}, f32[12,8,8,128]{3,2,1,0:T(8,128)}, f32[48,8,8,128]{3,2,1,0:T(8,128)S(1)}) custom-call(s32[6]{0:T(128)S(1)} %stack.148.refs_0_, f32[33]{0:T(128)S(1)} %get-tuple-element.825.refs_1_, f32[20,8,8,128]{3,2,1,0:T(8,128)} %get-tuple-element.755.refs_2_, f32[12,8,8,128]{3,2,1,0:T(8,128)S(1)} %copy-done.7, ...), custom_call_target="tpu_custom_call" | custom-call | flops 13107200 | bytes 6291456 | tf_op jit(solution)/shard_map/while/body/eval_jaxpr/u_block1/pallas_call | solution.py:391
  258.5 9.7 %l_block1.11 = (f32[20,8,8,128]{3,2,1,0:T(8,128)}, f32[12,8,8,128]{3,2,1,0:T(8,128)}, f32[24,8,8,128]{3,2,1,0:T(8,128)}) custom-call(s32[6]{0:T(128)S(1)} %stack.148.refs_0_, s32[2048]{0:T(1024)S(1)} %get-tuple-element.827.refs_1_, s32[2048]{0:T(1024)S(1)} %get-tuple-element.828.refs_2_, s32[7]{0:T(128)S(1)} %get-tuple-element.829.refs_3_, ...), custom_call_target="tpu_custom_call" | custom-call | flops 13107200 | bytes 6291456 | tf_op jit(solution)/shard_map/while/body/eval_jaxpr/l_block1/pallas_call | solution.py:407
  268.3 5.1 %collective-permute-start.2 = (f32[20,8,8,128]{3,2,1,0:T(8,128)}, f32[20,8,8,128]{3,2,1,0:T(8,128)S(1)}, u32[]{:S(2)}, u32[]{:S(2)}) collective-permute-start(f32[20,8,8,128]{3,2,1,0:T(8,128)} %get-tuple-element.795.refs_5_), channel_id=1, source_target_pairs={{0,1},{1,2},{2,3},{3,4},{4,5},{5,6},{6,7},{7,8},{8,9},{9,10},{10,1... | collective-permute-start | bytes 1966088 | tf_op jit(solution)/shard_map/while/body/eval_jaxpr/ppermute | solution.py:421
  273.5 6.1 %u_block0.11 = (f32[20,8,8,128]{3,2,1,0:T(8,128)}, f32[12,8,8,128]{3,2,1,0:T(8,128)S(1)}, f32[20,8,8,128]{3,2,1,0:T(8,128)S(1)}, f32[48,8,8,128]{3,2,1,0:T(8,128)S(1)}) custom-call(s32[6]{0:T(128)S(1)} %stack.149.refs_0_, f32[33]{0:T(128)S(1)} %get-tuple-element.825.refs_1_, f32[20,8,8,128]{3,2,1,0:T(8,128)} %get-tuple-element.792.refs_2_, ...), custom_call_target="tpu_custom_call" | custom-call | flops 13107200 | bytes 6291456 | tf_op jit(solution)/shard_map/while/body/eval_jaxpr/u_block0/pallas_call | solution.py:391
  285.1 8.9 %l_block0.11 = (f32[20,8,8,128]{3,2,1,0:T(8,128)S(1)}, f32[12,8,8,128]{3,2,1,0:T(8,128)S(1)}, f32[20,8,8,128]{3,2,1,0:T(8,128)S(1)}, f32[24,8,8,128]{3,2,1,0:T(8,128)S(1)}) custom-call(s32[6]{0:T(128)S(1)} %stack.149.refs_0_, s32[2048]{0:T(1024)S(1)} %get-tuple-element.827.refs_1_, s32[2048]{0:T(1024)S(1)} %get-tuple-element.828.refs_2_, ...), custom_call_target="tpu_custom_call" | custom-call | flops 13107200 | bytes 6291456 | tf_op jit(solution)/shard_map/while/body/eval_jaxpr/l_block0/pallas_call | solution.py:407
  296.8 6.1 %u_block1.11 = (f32[20,8,8,128]{3,2,1,0:T(8,128)}, f32[12,8,8,128]{3,2,1,0:T(8,128)}, f32[48,8,8,128]{3,2,1,0:T(8,128)S(1)}) custom-call(s32[6]{0:T(128)S(1)} %stack.148.refs_0_, f32[33]{0:T(128)S(1)} %get-tuple-element.825.refs_1_, f32[20,8,8,128]{3,2,1,0:T(8,128)} %get-tuple-element.755.refs_2_, f32[12,8,8,128]{3,2,1,0:T(8,128)S(1)} %copy-done.7, ...), custom_call_target="tpu_custom_call" | custom-call | flops 13107200 | bytes 6291456 | tf_op jit(solution)/shard_map/while/body/eval_jaxpr/u_block1/pallas_call | solution.py:391
  306.8 9.7 %l_block1.11 = (f32[20,8,8,128]{3,2,1,0:T(8,128)}, f32[12,8,8,128]{3,2,1,0:T(8,128)}, f32[24,8,8,128]{3,2,1,0:T(8,128)}) custom-call(s32[6]{0:T(128)S(1)} %stack.148.refs_0_, s32[2048]{0:T(1024)S(1)} %get-tuple-element.827.refs_1_, s32[2048]{0:T(1024)S(1)} %get-tuple-element.828.refs_2_, s32[7]{0:T(128)S(1)} %get-tuple-element.829.refs_3_, ...), custom_call_target="tpu_custom_call" | custom-call | flops 13107200 | bytes 6291456 | tf_op jit(solution)/shard_map/while/body/eval_jaxpr/l_block1/pallas_call | solution.py:407
  316.5 5.1 %collective-permute-start.2 = (f32[20,8,8,128]{3,2,1,0:T(8,128)}, f32[20,8,8,128]{3,2,1,0:T(8,128)S(1)}, u32[]{:S(2)}, u32[]{:S(2)}) collective-permute-start(f32[20,8,8,128]{3,2,1,0:T(8,128)} %get-tuple-element.795.refs_5_), channel_id=1, source_target_pairs={{0,1},{1,2},{2,3},{3,4},{4,5},{5,6},{6,7},{7,8},{8,9},{9,10},{10,1... | collective-permute-start | bytes 1966088 | tf_op jit(solution)/shard_map/while/body/eval_jaxpr/ppermute | solution.py:421
  321.7 6.1 %u_block0.11 = (f32[20,8,8,128]{3,2,1,0:T(8,128)}, f32[12,8,8,128]{3,2,1,0:T(8,128)S(1)}, f32[20,8,8,128]{3,2,1,0:T(8,128)S(1)}, f32[48,8,8,128]{3,2,1,0:T(8,128)S(1)}) custom-call(s32[6]{0:T(128)S(1)} %stack.149.refs_0_, f32[33]{0:T(128)S(1)} %get-tuple-element.825.refs_1_, f32[20,8,8,128]{3,2,1,0:T(8,128)} %get-tuple-element.792.refs_2_, ...), custom_call_target="tpu_custom_call" | custom-call | flops 13107200 | bytes 6291456 | tf_op jit(solution)/shard_map/while/body/eval_jaxpr/u_block0/pallas_call | solution.py:391
  333.3 8.9 %l_block0.11 = (f32[20,8,8,128]{3,2,1,0:T(8,128)S(1)}, f32[12,8,8,128]{3,2,1,0:T(8,128)S(1)}, f32[20,8,8,128]{3,2,1,0:T(8,128)S(1)}, f32[24,8,8,128]{3,2,1,0:T(8,128)S(1)}) custom-call(s32[6]{0:T(128)S(1)} %stack.149.refs_0_, s32[2048]{0:T(1024)S(1)} %get-tuple-element.827.refs_1_, s32[2048]{0:T(1024)S(1)} %get-tuple-element.828.refs_2_, ...), custom_call_target="tpu_custom_call" | custom-call | flops 13107200 | bytes 6291456 | tf_op jit(solution)/shard_map/while/body/eval_jaxpr/l_block0/pallas_call | solution.py:407
  345.0 6.1 %u_block1.11 = (f32[20,8,8,128]{3,2,1,0:T(8,128)}, f32[12,8,8,128]{3,2,1,0:T(8,128)}, f32[48,8,8,128]{3,2,1,0:T(8,128)S(1)}) custom-call(s32[6]{0:T(128)S(1)} %stack.148.refs_0_, f32[33]{0:T(128)S(1)} %get-tuple-element.825.refs_1_, f32[20,8,8,128]{3,2,1,0:T(8,128)} %get-tuple-element.755.refs_2_, f32[12,8,8,128]{3,2,1,0:T(8,128)S(1)} %copy-done.7, ...), custom_call_target="tpu_custom_call" | custom-call | flops 13107200 | bytes 6291456 | tf_op jit(solution)/shard_map/while/body/eval_jaxpr/u_block1/pallas_call | solution.py:391
  351.1 8.7 %collective-permute-start.1 = (f32[20,8,8,128]{3,2,1,0:T(8,128)}, f32[20,8,8,128]{3,2,1,0:T(8,128)}, u32[]{:S(2)}, u32[]{:S(2)}) collective-permute-start(f32[20,8,8,128]{3,2,1,0:T(8,128)} %get-tuple-element.814), channel_id=1, source_target_pairs={{0,1},{1,2},{2,3},{3,4},{4,5},{5,6},{6,7},{7,8},{8,9},{9,10},{10,1... | collective-permute-start | bytes 1966088 | tf_op jit(solution)/shard_map/while/body/eval_jaxpr/ppermute | solution.py:427
  360.9 9.7 %l_block1.11 = (f32[20,8,8,128]{3,2,1,0:T(8,128)}, f32[12,8,8,128]{3,2,1,0:T(8,128)}, f32[24,8,8,128]{3,2,1,0:T(8,128)}) custom-call(s32[6]{0:T(128)S(1)} %stack.148.refs_0_, s32[2048]{0:T(1024)S(1)} %get-tuple-element.827.refs_1_, s32[2048]{0:T(1024)S(1)} %get-tuple-element.828.refs_2_, s32[7]{0:T(128)S(1)} %get-tuple-element.829.refs_3_, ...), custom_call_target="tpu_custom_call" | custom-call | flops 13107200 | bytes 6291456 | tf_op jit(solution)/shard_map/while/body/eval_jaxpr/l_block1/pallas_call | solution.py:407
  370.6 7.8 %collective-permute-start.2 = (f32[20,8,8,128]{3,2,1,0:T(8,128)}, f32[20,8,8,128]{3,2,1,0:T(8,128)S(1)}, u32[]{:S(2)}, u32[]{:S(2)}) collective-permute-start(f32[20,8,8,128]{3,2,1,0:T(8,128)} %get-tuple-element.795.refs_5_), channel_id=1, source_target_pairs={{0,1},{1,2},{2,3},{3,4},{4,5},{5,6},{6,7},{7,8},{8,9},{9,10},{10,1... | collective-permute-start | bytes 1966088 | tf_op jit(solution)/shard_map/while/body/eval_jaxpr/ppermute | solution.py:421
  378.5 6.1 %u_block0.11 = (f32[20,8,8,128]{3,2,1,0:T(8,128)}, f32[12,8,8,128]{3,2,1,0:T(8,128)S(1)}, f32[20,8,8,128]{3,2,1,0:T(8,128)S(1)}, f32[48,8,8,128]{3,2,1,0:T(8,128)S(1)}) custom-call(s32[6]{0:T(128)S(1)} %stack.149.refs_0_, f32[33]{0:T(128)S(1)} %get-tuple-element.825.refs_1_, f32[20,8,8,128]{3,2,1,0:T(8,128)} %get-tuple-element.792.refs_2_, ...), custom_call_target="tpu_custom_call" | custom-call | flops 13107200 | bytes 6291456 | tf_op jit(solution)/shard_map/while/body/eval_jaxpr/u_block0/pallas_call | solution.py:391
  390.2 8.9 %l_block0.11 = (f32[20,8,8,128]{3,2,1,0:T(8,128)S(1)}, f32[12,8,8,128]{3,2,1,0:T(8,128)S(1)}, f32[20,8,8,128]{3,2,1,0:T(8,128)S(1)}, f32[24,8,8,128]{3,2,1,0:T(8,128)S(1)}) custom-call(s32[6]{0:T(128)S(1)} %stack.149.refs_0_, s32[2048]{0:T(1024)S(1)} %get-tuple-element.827.refs_1_, s32[2048]{0:T(1024)S(1)} %get-tuple-element.828.refs_2_, ...), custom_call_target="tpu_custom_call" | custom-call | flops 13107200 | bytes 6291456 | tf_op jit(solution)/shard_map/while/body/eval_jaxpr/l_block0/pallas_call | solution.py:407
  401.8 5.2 %u_block1.11 = (f32[20,8,8,128]{3,2,1,0:T(8,128)}, f32[12,8,8,128]{3,2,1,0:T(8,128)}, f32[48,8,8,128]{3,2,1,0:T(8,128)S(1)}) custom-call(s32[6]{0:T(128)S(1)} %stack.148.refs_0_, f32[33]{0:T(128)S(1)} %get-tuple-element.825.refs_1_, f32[20,8,8,128]{3,2,1,0:T(8,128)} %get-tuple-element.755.refs_2_, f32[12,8,8,128]{3,2,1,0:T(8,128)S(1)} %copy-done.7, ...), custom_call_target="tpu_custom_call" | custom-call | flops 13107200 | bytes 6291456 | tf_op jit(solution)/shard_map/while/body/eval_jaxpr/u_block1/pallas_call | solution.py:391
  409.9 7.0 %collective-permute-done.3.refs_7_ = f32[20,8,8,128]{3,2,1,0:T(8,128)} collective-permute-done((f32[20,8,8,128]{3,2,1,0:T(8,128)S(1)}, f32[20,8,8,128]{3,2,1,0:T(8,128)}, u32[]{:S(2)}, u32[]{:S(2)}) %collective-permute-start.3) | collective-permute-done | bytes 655392 | tf_op jit(solution)/shard_map/while/body/eval_jaxpr/ppermute | solution.py:425
  418.0 8.3 %l_block1.11 = (f32[20,8,8,128]{3,2,1,0:T(8,128)}, f32[12,8,8,128]{3,2,1,0:T(8,128)}, f32[24,8,8,128]{3,2,1,0:T(8,128)}) custom-call(s32[6]{0:T(128)S(1)} %stack.148.refs_0_, s32[2048]{0:T(1024)S(1)} %get-tuple-element.827.refs_1_, s32[2048]{0:T(1024)S(1)} %get-tuple-element.828.refs_2_, s32[7]{0:T(128)S(1)} %get-tuple-element.829.refs_3_, ...), custom_call_target="tpu_custom_call" | custom-call | flops 13107200 | bytes 6291456 | tf_op jit(solution)/shard_map/while/body/eval_jaxpr/l_block1/pallas_call | solution.py:407
  427.4 4.4 collective-permute-start.6
  431.8 3.8 collective-permute-done.6
  439.6 24.8 %reduce-scatter.2.cloned.1.call-done = f32[16,32,128]{2,1,0:T(8,128)} async-done(((f32[16,64,128]{2,1,0:T(8,128)}), f32[16,32,128]{2,1,0:T(8,128)}) %reduce-scatter.2.cloned.1.call-update) | async-done | bytes 262160 | tf_op jit(solution)/shard_map/reduce_scatter | solution.py:438
  (250 shorter events, 114.0 us)
Async XLA Ops:
  7.2 457.2 %reduce-scatter.2.cloned.1.call-start = ((), (), s32[]{:S(2)}) async-start(), calls=%async_computation.1 | async-start | bytes 786432 | tf_op jit(solution)/shard_map/reduce_scatter | solution.py:438
  9.6 12.6 %copy-start.13 = (f32[1,32,2048]{2,1,0:T(8,128)S(1)}, f32[1,32,2048]{2,1,0:T(8,128)}, u32[]{:S(2)}) copy-start(f32[1,32,2048]{2,1,0:T(8,128)} %param.15) | copy-start | bytes 786436
  12.2 15.9 %collective-permute-start.4 = (f32[20,8,8,128]{3,2,1,0:T(8,128)}, f32[20,8,8,128]{3,2,1,0:T(8,128)}, u32[]{:S(2)}, u32[]{:S(2)}) collective-permute-start(f32[20,8,8,128]{3,2,1,0:T(8,128)} %get-tuple-element.770), channel_id=1, source_target_pairs={{0,1},{1,2},{2,3},{3,4},{4,5},{5,6},{6,7},{7,8},{8,9},{9,10},{10,1... | collective-permute-start | bytes 1966088 | tf_op jit(solution)/shard_map/ppermute | solution.py:431
  14.1 13.0 %collective-permute-start.5 = (f32[8,64,128]{2,1,0:T(8,128)S(1)}, f32[8,64,128]{2,1,0:T(8,128)S(1)}, u32[]{:S(2)}, u32[]{:S(2)}) collective-permute-start(f32[8,64,128]{2,1,0:T(8,128)S(1)} %slice.18), channel_id=1, source_target_pairs={{0,1},{1,2},{2,3},{3,4},{4,5},{5,6},{6,7},{7,8},{8,9},{9,10},{10,1... | collective-permute-start | bytes 786440 | tf_op jit(solution)/shard_map/ppermute | solution.py:309
  28.1 403.7 %copy-start.14 = (s32[1,64,128]{2,1,0:T(8,128)S(1)}, s32[1,64,128]{2,1,0:T(8,128)}, u32[]{:S(2)}) copy-start(s32[1,64,128]{2,1,0:T(8,128)} %param.12) | copy-start | bytes 98308
  28.1 13.5 %collective-permute-start.2 = (f32[20,8,8,128]{3,2,1,0:T(8,128)}, f32[20,8,8,128]{3,2,1,0:T(8,128)S(1)}, u32[]{:S(2)}, u32[]{:S(2)}) collective-permute-start(f32[20,8,8,128]{3,2,1,0:T(8,128)} %get-tuple-element.795.refs_5_), channel_id=1, source_target_pairs={{0,1},{1,2},{2,3},{3,4},{4,5},{5,6},{6,7},{7,8},{8,9},{9,10},{10,1... | collective-permute-start | bytes 1966088 | tf_op jit(solution)/shard_map/while/body/eval_jaxpr/ppermute | solution.py:421
  37.9 17.6 %collective-permute-start = (f32[20,8,8,128]{3,2,1,0:T(8,128)}, f32[20,8,8,128]{3,2,1,0:T(8,128)}, u32[]{:S(2)}, u32[]{:S(2)}) collective-permute-start(f32[20,8,8,128]{3,2,1,0:T(8,128)} %get-tuple-element.755.refs_2_), channel_id=1, source_target_pairs={{1,0},{2,1},{3,2},{4,3},{5,4},{6,5},{7,6},{8,7},{9,8},{10,9},{11,1... | collective-permute-start | bytes 1966088 | tf_op jit(solution)/shard_map/while/body/eval_jaxpr/ppermute | solution.py:423
  43.6 11.9 %copy-start.3 = (f32[20,8,8,128]{3,2,1,0:T(8,128)S(1)}, f32[20,8,8,128]{3,2,1,0:T(8,128)}, u32[]{:S(2)}) copy-start(f32[20,8,8,128]{3,2,1,0:T(8,128)} %copy-done.2) | copy-start | bytes 1966084 | tf_op jit(solution)/shard_map/while
  43.6 12.0 %copy-start.7 = (f32[12,8,8,128]{3,2,1,0:T(8,128)S(1)}, f32[12,8,8,128]{3,2,1,0:T(8,128)}, u32[]{:S(2)}) copy-start(f32[12,8,8,128]{3,2,1,0:T(8,128)} %copy-done.6) | copy-start | bytes 1179652 | tf_op jit(solution)/shard_map/while
  53.3 11.2 %collective-permute-start.3 = (f32[20,8,8,128]{3,2,1,0:T(8,128)S(1)}, f32[20,8,8,128]{3,2,1,0:T(8,128)}, u32[]{:S(2)}, u32[]{:S(2)}) collective-permute-start(f32[20,8,8,128]{3,2,1,0:T(8,128)S(1)} %get-tuple-element.761.refs_5_), channel_id=1, source_target_pairs={{1,0},{2,1},{3,2},{4,3},{5,4},{6,5},{7,6},{8,7},{9,8},{10,9},{11,1... | collective-permute-start | bytes 1966088 | tf_op jit(solution)/shard_map/while/body/eval_jaxpr/ppermute | solution.py:425
  61.6 13.7 %collective-permute-start.1 = (f32[20,8,8,128]{3,2,1,0:T(8,128)}, f32[20,8,8,128]{3,2,1,0:T(8,128)}, u32[]{:S(2)}, u32[]{:S(2)}) collective-permute-start(f32[20,8,8,128]{3,2,1,0:T(8,128)} %get-tuple-element.814), channel_id=1, source_target_pairs={{0,1},{1,2},{2,3},{3,4},{4,5},{5,6},{6,7},{7,8},{8,9},{9,10},{10,1... | collective-permute-start | bytes 1966088 | tf_op jit(solution)/shard_map/while/body/eval_jaxpr/ppermute | solution.py:427
  75.3 14.8 %collective-permute-start.2 = (f32[20,8,8,128]{3,2,1,0:T(8,128)}, f32[20,8,8,128]{3,2,1,0:T(8,128)S(1)}, u32[]{:S(2)}, u32[]{:S(2)}) collective-permute-start(f32[20,8,8,128]{3,2,1,0:T(8,128)} %get-tuple-element.795.refs_5_), channel_id=1, source_target_pairs={{0,1},{1,2},{2,3},{3,4},{4,5},{5,6},{6,7},{7,8},{8,9},{9,10},{10,1... | collective-permute-start | bytes 1966088 | tf_op jit(solution)/shard_map/while/body/eval_jaxpr/ppermute | solution.py:421
  88.1 15.6 %collective-permute-start = (f32[20,8,8,128]{3,2,1,0:T(8,128)}, f32[20,8,8,128]{3,2,1,0:T(8,128)}, u32[]{:S(2)}, u32[]{:S(2)}) collective-permute-start(f32[20,8,8,128]{3,2,1,0:T(8,128)} %get-tuple-element.755.refs_2_), channel_id=1, source_target_pairs={{1,0},{2,1},{3,2},{4,3},{5,4},{6,5},{7,6},{8,7},{9,8},{10,9},{11,1... | collective-permute-start | bytes 1966088 | tf_op jit(solution)/shard_map/while/body/eval_jaxpr/ppermute | solution.py:423
  92.1 11.7 %copy-start.7 = (f32[12,8,8,128]{3,2,1,0:T(8,128)S(1)}, f32[12,8,8,128]{3,2,1,0:T(8,128)}, u32[]{:S(2)}) copy-start(f32[12,8,8,128]{3,2,1,0:T(8,128)} %copy-done.6) | copy-start | bytes 1179652 | tf_op jit(solution)/shard_map/while
  101.8 10.9 %collective-permute-start.3 = (f32[20,8,8,128]{3,2,1,0:T(8,128)S(1)}, f32[20,8,8,128]{3,2,1,0:T(8,128)}, u32[]{:S(2)}, u32[]{:S(2)}) collective-permute-start(f32[20,8,8,128]{3,2,1,0:T(8,128)S(1)} %get-tuple-element.761.refs_5_), channel_id=1, source_target_pairs={{1,0},{2,1},{3,2},{4,3},{5,4},{6,5},{7,6},{8,7},{9,8},{10,9},{11,1... | collective-permute-start | bytes 1966088 | tf_op jit(solution)/shard_map/while/body/eval_jaxpr/ppermute | solution.py:425
  109.8 13.7 %collective-permute-start.1 = (f32[20,8,8,128]{3,2,1,0:T(8,128)}, f32[20,8,8,128]{3,2,1,0:T(8,128)}, u32[]{:S(2)}, u32[]{:S(2)}) collective-permute-start(f32[20,8,8,128]{3,2,1,0:T(8,128)} %get-tuple-element.814), channel_id=1, source_target_pairs={{0,1},{1,2},{2,3},{3,4},{4,5},{5,6},{6,7},{7,8},{8,9},{9,10},{10,1... | collective-permute-start | bytes 1966088 | tf_op jit(solution)/shard_map/while/body/eval_jaxpr/ppermute | solution.py:427
  123.5 14.9 %collective-permute-start.2 = (f32[20,8,8,128]{3,2,1,0:T(8,128)}, f32[20,8,8,128]{3,2,1,0:T(8,128)S(1)}, u32[]{:S(2)}, u32[]{:S(2)}) collective-permute-start(f32[20,8,8,128]{3,2,1,0:T(8,128)} %get-tuple-element.795.refs_5_), channel_id=1, source_target_pairs={{0,1},{1,2},{2,3},{3,4},{4,5},{5,6},{6,7},{7,8},{8,9},{9,10},{10,1... | collective-permute-start | bytes 1966088 | tf_op jit(solution)/shard_map/while/body/eval_jaxpr/ppermute | solution.py:421
  136.4 15.6 %collective-permute-start = (f32[20,8,8,128]{3,2,1,0:T(8,128)}, f32[20,8,8,128]{3,2,1,0:T(8,128)}, u32[]{:S(2)}, u32[]{:S(2)}) collective-permute-start(f32[20,8,8,128]{3,2,1,0:T(8,128)} %get-tuple-element.755.refs_2_), channel_id=1, source_target_pairs={{1,0},{2,1},{3,2},{4,3},{5,4},{6,5},{7,6},{8,7},{9,8},{10,9},{11,1... | collective-permute-start | bytes 1966088 | tf_op jit(solution)/shard_map/while/body/eval_jaxpr/ppermute | solution.py:423
  140.3 11.7 %copy-start.7 = (f32[12,8,8,128]{3,2,1,0:T(8,128)S(1)}, f32[12,8,8,128]{3,2,1,0:T(8,128)}, u32[]{:S(2)}) copy-start(f32[12,8,8,128]{3,2,1,0:T(8,128)} %copy-done.6) | copy-start | bytes 1179652 | tf_op jit(solution)/shard_map/while
  150.0 10.9 %collective-permute-start.3 = (f32[20,8,8,128]{3,2,1,0:T(8,128)S(1)}, f32[20,8,8,128]{3,2,1,0:T(8,128)}, u32[]{:S(2)}, u32[]{:S(2)}) collective-permute-start(f32[20,8,8,128]{3,2,1,0:T(8,128)S(1)} %get-tuple-element.761.refs_5_), channel_id=1, source_target_pairs={{1,0},{2,1},{3,2},{4,3},{5,4},{6,5},{7,6},{8,7},{9,8},{10,9},{11,1... | collective-permute-start | bytes 1966088 | tf_op jit(solution)/shard_map/while/body/eval_jaxpr/ppermute | solution.py:425
  158.1 13.7 %collective-permute-start.1 = (f32[20,8,8,128]{3,2,1,0:T(8,128)}, f32[20,8,8,128]{3,2,1,0:T(8,128)}, u32[]{:S(2)}, u32[]{:S(2)}) collective-permute-start(f32[20,8,8,128]{3,2,1,0:T(8,128)} %get-tuple-element.814), channel_id=1, source_target_pairs={{0,1},{1,2},{2,3},{3,4},{4,5},{5,6},{6,7},{7,8},{8,9},{9,10},{10,1... | collective-permute-start | bytes 1966088 | tf_op jit(solution)/shard_map/while/body/eval_jaxpr/ppermute | solution.py:427
  171.8 14.9 %collective-permute-start.2 = (f32[20,8,8,128]{3,2,1,0:T(8,128)}, f32[20,8,8,128]{3,2,1,0:T(8,128)S(1)}, u32[]{:S(2)}, u32[]{:S(2)}) collective-permute-start(f32[20,8,8,128]{3,2,1,0:T(8,128)} %get-tuple-element.795.refs_5_), channel_id=1, source_target_pairs={{0,1},{1,2},{2,3},{3,4},{4,5},{5,6},{6,7},{7,8},{8,9},{9,10},{10,1... | collective-permute-start | bytes 1966088 | tf_op jit(solution)/shard_map/while/body/eval_jaxpr/ppermute | solution.py:421
  184.6 15.6 %collective-permute-start = (f32[20,8,8,128]{3,2,1,0:T(8,128)}, f32[20,8,8,128]{3,2,1,0:T(8,128)}, u32[]{:S(2)}, u32[]{:S(2)}) collective-permute-start(f32[20,8,8,128]{3,2,1,0:T(8,128)} %get-tuple-element.755.refs_2_), channel_id=1, source_target_pairs={{1,0},{2,1},{3,2},{4,3},{5,4},{6,5},{7,6},{8,7},{9,8},{10,9},{11,1... | collective-permute-start | bytes 1966088 | tf_op jit(solution)/shard_map/while/body/eval_jaxpr/ppermute | solution.py:423
  188.6 11.7 %copy-start.7 = (f32[12,8,8,128]{3,2,1,0:T(8,128)S(1)}, f32[12,8,8,128]{3,2,1,0:T(8,128)}, u32[]{:S(2)}) copy-start(f32[12,8,8,128]{3,2,1,0:T(8,128)} %copy-done.6) | copy-start | bytes 1179652 | tf_op jit(solution)/shard_map/while
  198.3 10.9 %collective-permute-start.3 = (f32[20,8,8,128]{3,2,1,0:T(8,128)S(1)}, f32[20,8,8,128]{3,2,1,0:T(8,128)}, u32[]{:S(2)}, u32[]{:S(2)}) collective-permute-start(f32[20,8,8,128]{3,2,1,0:T(8,128)S(1)} %get-tuple-element.761.refs_5_), channel_id=1, source_target_pairs={{1,0},{2,1},{3,2},{4,3},{5,4},{6,5},{7,6},{8,7},{9,8},{10,9},{11,1... | collective-permute-start | bytes 1966088 | tf_op jit(solution)/shard_map/while/body/eval_jaxpr/ppermute | solution.py:425
  206.3 13.7 %collective-permute-start.1 = (f32[20,8,8,128]{3,2,1,0:T(8,128)}, f32[20,8,8,128]{3,2,1,0:T(8,128)}, u32[]{:S(2)}, u32[]{:S(2)}) collective-permute-start(f32[20,8,8,128]{3,2,1,0:T(8,128)} %get-tuple-element.814), channel_id=1, source_target_pairs={{0,1},{1,2},{2,3},{3,4},{4,5},{5,6},{6,7},{7,8},{8,9},{9,10},{10,1... | collective-permute-start | bytes 1966088 | tf_op jit(solution)/shard_map/while/body/eval_jaxpr/ppermute | solution.py:427
  220.0 14.9 %collective-permute-start.2 = (f32[20,8,8,128]{3,2,1,0:T(8,128)}, f32[20,8,8,128]{3,2,1,0:T(8,128)S(1)}, u32[]{:S(2)}, u32[]{:S(2)}) collective-permute-start(f32[20,8,8,128]{3,2,1,0:T(8,128)} %get-tuple-element.795.refs_5_), channel_id=1, source_target_pairs={{0,1},{1,2},{2,3},{3,4},{4,5},{5,6},{6,7},{7,8},{8,9},{9,10},{10,1... | collective-permute-start | bytes 1966088 | tf_op jit(solution)/shard_map/while/body/eval_jaxpr/ppermute | solution.py:421
  232.9 15.6 %collective-permute-start = (f32[20,8,8,128]{3,2,1,0:T(8,128)}, f32[20,8,8,128]{3,2,1,0:T(8,128)}, u32[]{:S(2)}, u32[]{:S(2)}) collective-permute-start(f32[20,8,8,128]{3,2,1,0:T(8,128)} %get-tuple-element.755.refs_2_), channel_id=1, source_target_pairs={{1,0},{2,1},{3,2},{4,3},{5,4},{6,5},{7,6},{8,7},{9,8},{10,9},{11,1... | collective-permute-start | bytes 1966088 | tf_op jit(solution)/shard_map/while/body/eval_jaxpr/ppermute | solution.py:423
  236.8 11.7 %copy-start.7 = (f32[12,8,8,128]{3,2,1,0:T(8,128)S(1)}, f32[12,8,8,128]{3,2,1,0:T(8,128)}, u32[]{:S(2)}) copy-start(f32[12,8,8,128]{3,2,1,0:T(8,128)} %copy-done.6) | copy-start | bytes 1179652 | tf_op jit(solution)/shard_map/while
  246.6 10.9 %collective-permute-start.3 = (f32[20,8,8,128]{3,2,1,0:T(8,128)S(1)}, f32[20,8,8,128]{3,2,1,0:T(8,128)}, u32[]{:S(2)}, u32[]{:S(2)}) collective-permute-start(f32[20,8,8,128]{3,2,1,0:T(8,128)S(1)} %get-tuple-element.761.refs_5_), channel_id=1, source_target_pairs={{1,0},{2,1},{3,2},{4,3},{5,4},{6,5},{7,6},{8,7},{9,8},{10,9},{11,1... | collective-permute-start | bytes 1966088 | tf_op jit(solution)/shard_map/while/body/eval_jaxpr/ppermute | solution.py:425
  254.6 13.7 %collective-permute-start.1 = (f32[20,8,8,128]{3,2,1,0:T(8,128)}, f32[20,8,8,128]{3,2,1,0:T(8,128)}, u32[]{:S(2)}, u32[]{:S(2)}) collective-permute-start(f32[20,8,8,128]{3,2,1,0:T(8,128)} %get-tuple-element.814), channel_id=1, source_target_pairs={{0,1},{1,2},{2,3},{3,4},{4,5},{5,6},{6,7},{7,8},{8,9},{9,10},{10,1... | collective-permute-start | bytes 1966088 | tf_op jit(solution)/shard_map/while/body/eval_jaxpr/ppermute | solution.py:427
  268.3 14.9 %collective-permute-start.2 = (f32[20,8,8,128]{3,2,1,0:T(8,128)}, f32[20,8,8,128]{3,2,1,0:T(8,128)S(1)}, u32[]{:S(2)}, u32[]{:S(2)}) collective-permute-start(f32[20,8,8,128]{3,2,1,0:T(8,128)} %get-tuple-element.795.refs_5_), channel_id=1, source_target_pairs={{0,1},{1,2},{2,3},{3,4},{4,5},{5,6},{6,7},{7,8},{8,9},{9,10},{10,1... | collective-permute-start | bytes 1966088 | tf_op jit(solution)/shard_map/while/body/eval_jaxpr/ppermute | solution.py:421
  281.1 15.6 %collective-permute-start = (f32[20,8,8,128]{3,2,1,0:T(8,128)}, f32[20,8,8,128]{3,2,1,0:T(8,128)}, u32[]{:S(2)}, u32[]{:S(2)}) collective-permute-start(f32[20,8,8,128]{3,2,1,0:T(8,128)} %get-tuple-element.755.refs_2_), channel_id=1, source_target_pairs={{1,0},{2,1},{3,2},{4,3},{5,4},{6,5},{7,6},{8,7},{9,8},{10,9},{11,1... | collective-permute-start | bytes 1966088 | tf_op jit(solution)/shard_map/while/body/eval_jaxpr/ppermute | solution.py:423
  285.1 11.7 %copy-start.7 = (f32[12,8,8,128]{3,2,1,0:T(8,128)S(1)}, f32[12,8,8,128]{3,2,1,0:T(8,128)}, u32[]{:S(2)}) copy-start(f32[12,8,8,128]{3,2,1,0:T(8,128)} %copy-done.6) | copy-start | bytes 1179652 | tf_op jit(solution)/shard_map/while
  294.8 10.9 %collective-permute-start.3 = (f32[20,8,8,128]{3,2,1,0:T(8,128)S(1)}, f32[20,8,8,128]{3,2,1,0:T(8,128)}, u32[]{:S(2)}, u32[]{:S(2)}) collective-permute-start(f32[20,8,8,128]{3,2,1,0:T(8,128)S(1)} %get-tuple-element.761.refs_5_), channel_id=1, source_target_pairs={{1,0},{2,1},{3,2},{4,3},{5,4},{6,5},{7,6},{8,7},{9,8},{10,9},{11,1... | collective-permute-start | bytes 1966088 | tf_op jit(solution)/shard_map/while/body/eval_jaxpr/ppermute | solution.py:425
  302.8 13.7 %collective-permute-start.1 = (f32[20,8,8,128]{3,2,1,0:T(8,128)}, f32[20,8,8,128]{3,2,1,0:T(8,128)}, u32[]{:S(2)}, u32[]{:S(2)}) collective-permute-start(f32[20,8,8,128]{3,2,1,0:T(8,128)} %get-tuple-element.814), channel_id=1, source_target_pairs={{0,1},{1,2},{2,3},{3,4},{4,5},{5,6},{6,7},{7,8},{8,9},{9,10},{10,1... | collective-permute-start | bytes 1966088 | tf_op jit(solution)/shard_map/while/body/eval_jaxpr/ppermute | solution.py:427
  316.5 14.9 %collective-permute-start.2 = (f32[20,8,8,128]{3,2,1,0:T(8,128)}, f32[20,8,8,128]{3,2,1,0:T(8,128)S(1)}, u32[]{:S(2)}, u32[]{:S(2)}) collective-permute-start(f32[20,8,8,128]{3,2,1,0:T(8,128)} %get-tuple-element.795.refs_5_), channel_id=1, source_target_pairs={{0,1},{1,2},{2,3},{3,4},{4,5},{5,6},{6,7},{7,8},{8,9},{9,10},{10,1... | collective-permute-start | bytes 1966088 | tf_op jit(solution)/shard_map/while/body/eval_jaxpr/ppermute | solution.py:421
  329.4 15.6 %collective-permute-start = (f32[20,8,8,128]{3,2,1,0:T(8,128)}, f32[20,8,8,128]{3,2,1,0:T(8,128)}, u32[]{:S(2)}, u32[]{:S(2)}) collective-permute-start(f32[20,8,8,128]{3,2,1,0:T(8,128)} %get-tuple-element.755.refs_2_), channel_id=1, source_target_pairs={{1,0},{2,1},{3,2},{4,3},{5,4},{6,5},{7,6},{8,7},{9,8},{10,9},{11,1... | collective-permute-start | bytes 1966088 | tf_op jit(solution)/shard_map/while/body/eval_jaxpr/ppermute | solution.py:423
  333.3 11.7 %copy-start.7 = (f32[12,8,8,128]{3,2,1,0:T(8,128)S(1)}, f32[12,8,8,128]{3,2,1,0:T(8,128)}, u32[]{:S(2)}) copy-start(f32[12,8,8,128]{3,2,1,0:T(8,128)} %copy-done.6) | copy-start | bytes 1179652 | tf_op jit(solution)/shard_map/while
  343.1 16.7 %collective-permute-start.3 = (f32[20,8,8,128]{3,2,1,0:T(8,128)S(1)}, f32[20,8,8,128]{3,2,1,0:T(8,128)}, u32[]{:S(2)}, u32[]{:S(2)}) collective-permute-start(f32[20,8,8,128]{3,2,1,0:T(8,128)S(1)} %get-tuple-element.761.refs_5_), channel_id=1, source_target_pairs={{1,0},{2,1},{3,2},{4,3},{5,4},{6,5},{7,6},{8,7},{9,8},{10,9},{11,1... | collective-permute-start | bytes 1966088 | tf_op jit(solution)/shard_map/while/body/eval_jaxpr/ppermute | solution.py:425
  351.1 19.5 %collective-permute-start.1 = (f32[20,8,8,128]{3,2,1,0:T(8,128)}, f32[20,8,8,128]{3,2,1,0:T(8,128)}, u32[]{:S(2)}, u32[]{:S(2)}) collective-permute-start(f32[20,8,8,128]{3,2,1,0:T(8,128)} %get-tuple-element.814), channel_id=1, source_target_pairs={{0,1},{1,2},{2,3},{3,4},{4,5},{5,6},{6,7},{7,8},{8,9},{9,10},{10,1... | collective-permute-start | bytes 1966088 | tf_op jit(solution)/shard_map/while/body/eval_jaxpr/ppermute | solution.py:427
  370.6 17.6 %collective-permute-start.2 = (f32[20,8,8,128]{3,2,1,0:T(8,128)}, f32[20,8,8,128]{3,2,1,0:T(8,128)S(1)}, u32[]{:S(2)}, u32[]{:S(2)}) collective-permute-start(f32[20,8,8,128]{3,2,1,0:T(8,128)} %get-tuple-element.795.refs_5_), channel_id=1, source_target_pairs={{0,1},{1,2},{2,3},{3,4},{4,5},{5,6},{6,7},{7,8},{8,9},{9,10},{10,1... | collective-permute-start | bytes 1966088 | tf_op jit(solution)/shard_map/while/body/eval_jaxpr/ppermute | solution.py:421
  386.2 15.6 %collective-permute-start = (f32[20,8,8,128]{3,2,1,0:T(8,128)}, f32[20,8,8,128]{3,2,1,0:T(8,128)}, u32[]{:S(2)}, u32[]{:S(2)}) collective-permute-start(f32[20,8,8,128]{3,2,1,0:T(8,128)} %get-tuple-element.755.refs_2_), channel_id=1, source_target_pairs={{1,0},{2,1},{3,2},{4,3},{5,4},{6,5},{7,6},{8,7},{9,8},{10,9},{11,1... | collective-permute-start | bytes 1966088 | tf_op jit(solution)/shard_map/while/body/eval_jaxpr/ppermute | solution.py:423
  390.2 11.7 %copy-start.7 = (f32[12,8,8,128]{3,2,1,0:T(8,128)S(1)}, f32[12,8,8,128]{3,2,1,0:T(8,128)}, u32[]{:S(2)}) copy-start(f32[12,8,8,128]{3,2,1,0:T(8,128)} %copy-done.6) | copy-start | bytes 1179652 | tf_op jit(solution)/shard_map/while
  399.9 17.0 %collective-permute-start.3 = (f32[20,8,8,128]{3,2,1,0:T(8,128)S(1)}, f32[20,8,8,128]{3,2,1,0:T(8,128)}, u32[]{:S(2)}, u32[]{:S(2)}) collective-permute-start(f32[20,8,8,128]{3,2,1,0:T(8,128)S(1)} %get-tuple-element.761.refs_5_), channel_id=1, source_target_pairs={{1,0},{2,1},{3,2},{4,3},{5,4},{6,5},{7,6},{8,7},{9,8},{10,9},{11,1... | collective-permute-start | bytes 1966088 | tf_op jit(solution)/shard_map/while/body/eval_jaxpr/ppermute | solution.py:425
  407.1 19.2 %collective-permute-start.1 = (f32[20,8,8,128]{3,2,1,0:T(8,128)}, f32[20,8,8,128]{3,2,1,0:T(8,128)}, u32[]{:S(2)}, u32[]{:S(2)}) collective-permute-start(f32[20,8,8,128]{3,2,1,0:T(8,128)} %get-tuple-element.814), channel_id=1, source_target_pairs={{0,1},{1,2},{2,3},{3,4},{4,5},{5,6},{6,7},{7,8},{8,9},{9,10},{10,1... | collective-permute-start | bytes 1966088 | tf_op jit(solution)/shard_map/while/body/eval_jaxpr/ppermute | solution.py:427
  427.4 8.3 %collective-permute-start.6 = (f32[8,8,8,128]{3,2,1,0:T(8,128)S(1)}, f32[8,8,8,128]{3,2,1,0:T(8,128)S(1)}, u32[]{:S(2)}, u32[]{:S(2)}) collective-permute-start(f32[8,8,8,128]{3,2,1,0:T(8,128)S(1)} %get-tuple-element.629), channel_id=1, source_target_pairs={{1,0},{2,1},{3,2},{4,3},{5,4},{6,5},{7,6},{8,7},{9,8},{10,9},{11,1... | collective-permute-start | bytes 786440 | tf_op jit(solution)/shard_map/ppermute | solution.py:435
  437.6 26.8 %copy-start.10 = (f32[16,64,128]{2,1,0:T(8,128)S(1)}, f32[16,64,128]{2,1,0:T(8,128)}, u32[]{:S(2)}) copy-start(f32[16,64,128]{2,1,0:T(8,128)} %param.11) | copy-start | bytes 1572868
  (60 other events, 148.0 us)
Sparse Core Ops, SparseCore 0:
  437.7 26.6 reduce-scatter.1

commit v2 on v1

--- a/solution.py
+++ b/solution.py
@@ -7,11 +7,14 @@
 from jax.experimental.pallas import tpu as pltpu
 from jax.sharding import PartitionSpec as P
 
-COEFS = (-205.0 / 72.0, 8.0 / 5.0, -1.0 / 5.0, 8.0 / 315.0, -1.0 / 560.0)
+SCALE = 5040.0
+WHOLE = (-14350.0, 8064.0, -1008.0, 128.0, -9.0)
 REACH = 4
 SHIFT = 8
-VMEM_BYTES = 40 * 1024 * 1024
+VMEM_BYTES = 20 * 1024 * 1024
 SUB = 8
+PIECES = 3
+CHUNK = 256
 
 MSG = 2 * SHIFT + REACH
 REST = SHIFT + REACH
@@ -34,25 +37,42 @@
     return field.transpose(0, 2, 1, 3).reshape(layers, sub * parts, width_y)
 
 
+def split3(f):
+    hi = f.astype(jnp.bfloat16)
+    left = f - hi.astype(jnp.float32)
+    mid = left.astype(jnp.bfloat16)
+    return hi, mid, (left - mid.astype(jnp.float32)).astype(jnp.bfloat16)
+
+
+def lane_pass(cur, first, count, weights, pieces, ybuf):
+    parts, _, width_y = cur.shape[1:]
+    rows = parts * SUB
+
+    def one(q):
+        at = pl.multiple_of(q * rows, rows)
+        for i, piece in enumerate(split3(cur[first + q].reshape(rows, width_y))):
+            pieces[pl.ds(at, rows), i * width_y : (i + 1) * width_y] = piece
+
+    layers_loop(0, count, one)
+    for q in range(0, count, SHIFT):
+        block = slice(q * rows, min(q + SHIFT, count) * rows)
+        ybuf[block, :] = jnp.dot(pieces[block, :], weights[...], preferred_element_type=jnp.float32)
+
+
 def lap_maker(parts, width_y):
-    lane = lax.broadcasted_iota(jnp.int32, (1, SUB, width_y), 2)
     row = lax.broadcasted_iota(jnp.int32, (1, SUB, width_y), 1)
-    plus = [jnp.where(lane < width_y - k, COEFS[k], 0.0).astype(jnp.float32) for k in range(1, 5)]
-    minus = [jnp.where(lane >= k, COEFS[k], 0.0).astype(jnp.float32) for k in range(1, 5)]
-
-    def lap(ref, j):
+
+    def lap(ref, j, along):
         f = ref[j]
         after = jnp.where(row == SUB - 1, 0.0, pltpu.roll(f[:REACH], SUB - 1, 1))
         before = jnp.where(row == 0, 0.0, pltpu.roll(f[parts - REACH :], 1, 1))
         wide = jnp.concatenate([before, f, after], axis=0)
-        total = (3.0 * COEFS[0]) * f
+        total = along + (3.0 * WHOLE[0]) * f
         for k in range(1, 5):
             pair = (ref[j + k] + ref[j - k]) + (
                 wide[REACH + k : REACH + k + parts] + wide[REACH - k : REACH - k + parts]
             )
-            total = total + COEFS[k] * pair
-            total = total + plus[k - 1] * pltpu.roll(f, width_y - k, 2)
-            total = total + minus[k - 1] * pltpu.roll(f, k, 2)
+            total = total + WHOLE[k] * pair
         return f, total
 
     return lap
@@ -66,23 +86,91 @@
     lax.fori_loop(0, count, one, 0, unroll=2)
 
 
-def inject(rbuf, rl, ids, starts, res, level, first, last, bits, width_y):
-    lane = lax.broadcasted_iota(jnp.int32, (1, width_y), 1)
-
-    def one(r, carry):
-        place = rl[r]
-        who = ids[r]
-        row = lax.shift_right_logical(place, bits)
-        col = place & ((1 << bits) - 1)
-        value = res[level, lax.shift_right_logical(who, 7), who & 127]
-        spot = rbuf[pl.ds(row, 1), :]
-        rbuf[pl.ds(row, 1), :] = spot + jnp.where(lane == col, value, 0.0)
+def inject(rbuf, rows, starts, table, level, first, last):
+    low, high = starts[first], starts[last]
+
+    def eight(i, carry):
+        for q in range(8):
+            r = jnp.minimum(low + i * 8 + q, high - 1)
+            rbuf[pl.ds(rows[r], 1), :] = table[level, pl.ds(r, 1), :]
         return carry
 
-    lax.fori_loop(starts[first], starts[last], one, 0)
-
-
-def block_kernel(side, is_l, bits, *refs):
+    lax.fori_loop(0, (high - low + 7) // 8, eight, 0)
+
+
+def chunks_of(starts):
+    return (starts[starts.shape[0] - 1] + CHUNK - 1) // CHUNK
+
+
+def table_kernel(starts, ids, rows_l, rows_s, lanes_s, res, out, res_cut, pieces, same, part, sem):
+    steps, receivers = res.shape
+    width_y = part.shape[2]
+    chunks = chunks_of(starts)
+    for i, piece in enumerate(split3(res[...])):
+        pieces[i * steps : (i + 1) * steps, :] = piece
+
+    def column(c, carry):
+        who = lax.broadcasted_iota(jnp.int32, (receivers, CHUNK), 0) == ids[pl.ds(c, 1), :]
+        moved = jnp.dot(
+            pieces[...], jnp.where(who, 1.0, 0.0).astype(jnp.bfloat16), preferred_element_type=jnp.float32
+        )
+        total = (moved[:steps] + moved[steps : 2 * steps]) + moved[2 * steps :]
+        res_cut[c] = SCALE * total
+        return carry
+
+    lax.fori_loop(0, chunks, column, 0)
+
+    def to_chunk(c, carry):
+        mine = rows_s[pl.ds(pl.multiple_of(c * CHUNK, CHUNK), CHUNK), :]
+
+        def from_chunk(d, carry):
+            same[...] = jnp.where(mine == rows_l[pl.ds(d, 1), :], 1.0, 0.0)
+            at = pl.multiple_of(d * CHUNK, CHUNK)
+            lane = lax.broadcasted_iota(jnp.int32, (CHUNK, width_y), 1)
+            spots = jnp.where(lane == lanes_s[pl.ds(at, CHUNK), :], 1.0, 0.0).astype(jnp.bfloat16)
+
+            def one(n, carry):
+                total = jnp.zeros((CHUNK, width_y), jnp.float32)
+                for piece in split3(same[...] * res_cut[d, pl.ds(n, 1), :]):
+                    total = total + jnp.dot(piece, spots, preferred_element_type=jnp.float32)
+
+                @pl.when(d == 0)
+                def _():
+                    part[n] = total
+
+                @pl.when(d > 0)
+                def _():
+                    part[n] = part[n] + total
+
+                return carry
+
+            return lax.fori_loop(0, steps, one, carry)
+
+        lax.fori_loop(0, chunks, from_chunk, 0)
+        at = pl.multiple_of(c * CHUNK, CHUNK)
+        write = pltpu.make_async_copy(part, out.at[:, pl.ds(at, CHUNK), :], sem)
+        write.start()
+        write.wait()
+        return carry
+
+    lax.fori_loop(0, chunks, to_chunk, 0)
+
+
+def fetch_table(table_hbm, table, starts, sem, steps):
+    def each(act):
+        def one(c, carry):
+            at = pl.ds(pl.multiple_of(c * CHUNK, CHUNK), CHUNK)
+            for i, n in enumerate(steps):
+                act(pltpu.make_async_copy(table_hbm.at[n, at, :], table.at[i, at, :], sem.at[i, c]))
+            return carry
+
+        lax.fori_loop(0, chunks_of(starts), one, 0)
+
+    each(lambda copy: copy.start())
+    return lambda: each(lambda copy: copy.wait())
+
+
+def block_kernel(side, is_l, *refs):
     refs = list(refs)
 
     def take(count):
@@ -91,12 +179,12 @@
         return got
 
     (scal,) = take(1)
-    wave = rl = ids = starts = res_hbm = x_in = g_in = vmsg_in = None
-    if is_l:
-        rl, ids, starts, res_hbm = take(4)
+    wave = rows_of = starts = table_hbm = x_in = g_in = vmsg_in = None
+    if is_l:
+        rows_of, starts, table_hbm = take(3)
     else:
         (wave,) = take(1)
-    own, rest, recv, coef = take(4)
+    own, rest, recv, coef, weights = take(5)
     if side == 1:
         (vmsg_in,) = take(1)
     if is_l:
@@ -109,10 +197,10 @@
         (g,) = take(1)
     else:
         (x_out,) = take(1)
-    a, b, c, p = take(4)
-    rbuf = res = sem = None
-    if is_l:
-        rbuf, res, sem = take(3)
+    a, b, c, p, pieces, ybuf = take(6)
+    rbuf = table = sem = None
+    if is_l:
+        rbuf, table, sem = take(3)
 
     parts, _, width_y = a.shape[1:]
     rows = parts * SUB
@@ -121,8 +209,7 @@
     lap = lap_maker(parts, width_y)
 
     if is_l:
-        fetch = pltpu.make_async_copy(res_hbm.at[pl.ds(n0 - 1, 3)], res, sem)
-        fetch.start()
+        await_table = fetch_table(table_hbm, table, starts, sem, (n0, n0 - 1, jnp.maximum(n0 - 2, 0)))
         rbuf[...] = jnp.zeros(rbuf.shape, jnp.float32)
 
     def bring(msg, low):
@@ -162,7 +249,7 @@
             bring(recv, False)
 
     if is_l:
-        fetch.wait()
+        await_table()
 
     def source(nxt, level, first, count):
         j = src_layer + off
@@ -171,18 +258,20 @@
         def _():
             lane = lax.broadcasted_iota(jnp.int32, (1, width_y), 1)
             spot = nxt[j, src_part, pl.ds(src_row, 1), :]
-            gain = coef[src_layer, src_part, pl.ds(src_row, 1), :] * wave[n0 + 1 - level]
+            gain = coef[src_layer, src_part, pl.ds(src_row, 1), :] * wave[jnp.maximum(n0 - level, 0)]
             nxt[j, src_part, pl.ds(src_row, 1), :] = spot - jnp.where(lane == src_lane, gain, 0.0)
 
     def advance(level, cur, nxt, first, count, x_base, outs, x_save=None):
         if is_l:
             zone = (first - off) // REACH
-            inject(rbuf, rl, ids, starts, res, 2 - level, zone, zone + count // REACH, bits, width_y)
+            inject(rbuf, rows_of, starts, table, level, zone, zone + count // REACH)
         else:
             source(nxt, level, first, count)
+        lane_pass(cur, first, count, weights, pieces, ybuf)
 
         def body(j):
-            f, total = lap(cur, j)
+            y_at = pl.multiple_of((j - first) * rows, rows)
+            f, total = lap(cur, j, ybuf[pl.ds(y_at, rows), :].reshape(parts, SUB, width_y))
             if is_l:
                 at = pl.multiple_of((j - off) * rows, rows)
                 total = total + rbuf[pl.ds(at, rows), :].reshape(parts, SUB, width_y)
@@ -248,17 +337,20 @@
         msg_out[SHIFT + REACH : MSG] = jnp.zeros((SHIFT,) + a.shape[1:], jnp.float32)
 
 
-def first_u_kernel(scal, wave, f0, f1, coef, msg_out, rest_out):
+def first_u_kernel(scal, wave, f0, f1, coef, weights, msg_out, rest_out, pieces, ybuf):
     depth, parts, _, width_y = f0.shape
+    rows = parts * SUB
     n0, _, src_layer, src_part, src_row, src_lane = (scal[i] for i in range(6))
     lap = lap_maker(parts, width_y)
     msg_out[0:SHIFT] = f0[depth - SHIFT : depth]
     msg_out[SHIFT : SHIFT + REACH] = f1[depth - REACH : depth]
     rest_out[0:SHIFT] = f0[0:SHIFT]
     rest_out[SHIFT:REST] = f1[0:REACH]
+    lane_pass(f0, REACH, SHIFT, weights, pieces, ybuf)
 
     def body(j):
-        f, total = lap(f0, j)
+        y_at = pl.multiple_of((j - REACH) * rows, rows)
+        f, total = lap(f0, j, ybuf[pl.ds(y_at, rows), :].reshape(parts, SUB, width_y))
         msg_out[j + SHIFT] = (2.0 * f - f1[j]) + coef[j] * total
 
     layers_loop(REACH, SHIFT, body)
@@ -268,22 +360,21 @@
     def _():
         lane = lax.broadcasted_iota(jnp.int32, (1, width_y), 1)
         spot = msg_out[j + SHIFT, src_part, pl.ds(src_row, 1), :]
-        gain = coef[j, src_part, pl.ds(src_row, 1), :] * wave[n0 + 1]
+        gain = coef[j, src_part, pl.ds(src_row, 1), :] * wave[n0]
         msg_out[j + SHIFT, src_part, pl.ds(src_row, 1), :] = spot + jnp.where(lane == src_lane, gain, 0.0)
 
 
-def first_l_kernel(bits, scal, rl, ids, starts, res_hbm, f0, coef, msg_out, rest_out, g, rbuf, res, sem):
+def first_l_kernel(scal, rows_of, starts, table_hbm, f0, coef, msg_out, rest_out, g, rbuf, table, sem):
     depth, parts, _, width_y = f0.shape
     rows = parts * SUB
-    fetch = pltpu.make_async_copy(res_hbm.at[pl.ds(scal[0] - 1, 3)], res, sem)
-    fetch.start()
+    await_table = fetch_table(table_hbm, table, starts, sem, (scal[0],))
     rbuf[...] = jnp.zeros(rbuf.shape, jnp.float32)
     msg_out[0 : SHIFT + REACH] = jnp.zeros((SHIFT + REACH,) + f0.shape[1:], jnp.float32)
     rest_out[...] = jnp.zeros(rest_out.shape, jnp.float32)
     g[...] = jnp.zeros(g.shape, jnp.float32)
-    fetch.wait()
+    await_table()
     zone = (SHIFT + REACH) // REACH
-    inject(rbuf, rl, ids, starts, res, 2, zone, zone + SHIFT // REACH, bits, width_y)
+    inject(rbuf, rows_of, starts, table, 0, zone, zone + SHIFT // REACH)
 
     def body(j):
         at = pl.multiple_of((j + SHIFT) * rows, rows)
@@ -292,6 +383,25 @@
         g[j + SHIFT] = f0[j] * new
 
     layers_loop(REACH, SHIFT, body)
+
+
+def lane_weights(width_y):
+    away = jnp.abs(jnp.arange(width_y)[:, None] - jnp.arange(width_y)[None, :])
+    once = jnp.zeros((width_y, width_y), jnp.float32)
+    for k in range(1, 5):
+        once = jnp.where(away == k, WHOLE[k], once)
+    return jnp.tile(once.astype(jnp.bfloat16), (PIECES, 1))
+
+
+def sum_shots(g):
+    shots = lax.axis_size("shot")
+    if shots != 2:
+        return lax.psum_scatter(g, "shot", scatter_dimension=1, tiled=True)
+    block = g.shape[1] // 2
+    low, high = g[:, :block], g[:, block:]
+    first = lax.axis_index("shot") == 0
+    other = lax.ppermute(jnp.where(first, high, low), "shot", [(0, 1), (1, 0)])
+    return jnp.where(first, low, high) + other
 
 
 def on_device(fwd_last, fwd_prev, velocity, aperture, rec_index, src_index, residual):
@@ -303,12 +413,15 @@
     slab = lax.axis_index("slab")
     up = [(i, i + 1) for i in range(slabs - 1)]
     down = [(i + 1, i) for i in range(slabs - 1)]
-    bits = (width_y - 1).bit_length()
     f32 = jnp.float32
 
+    def coef_of(speed):
+        return tiled((0.4 * speed) ** 2 * (1.0 / SCALE))
+
     vel_left = lax.ppermute(velocity[depth - SHIFT :], "slab", up)
-    coef_own = tiled((0.4 * velocity) ** 2)
-    coef = jnp.concatenate([tiled((0.4 * vel_left) ** 2), coef_own], axis=0)
+    coef_own = coef_of(velocity)
+    coef = jnp.concatenate([coef_of(vel_left), coef_own], axis=0)
+    weights = lane_weights(width_y)
 
     base = (slab * depth - SHIFT) * plane
     window = (depth + SHIFT) * plane
@@ -323,7 +436,7 @@
         return layer, x % parts, x // parts, cell % width_y
 
     layer, part, row, lane = place_of(keys)
-    rl = (((layer * parts + part) * SUB + row) << bits) | lane
+    rows_of = (layer * parts + part) * SUB + row
     zones = (depth + SHIFT) // REACH
     edges = jnp.arange(zones + 1, dtype=jnp.int32) * (REACH * plane)
     starts = jnp.sum((keys[None, :] < edges[:, None]).astype(jnp.int32), axis=1)
@@ -337,10 +450,7 @@
     def scal_of(n0):
         return jnp.stack([jnp.asarray(n0, jnp.int32), is_last, s_layer, s_part, s_row, s_lane])
 
-    wave = jnp.concatenate([jnp.zeros((1,), f32), ricker(jnp.arange(total_steps, dtype=f32))])
-    res = jnp.concatenate([jnp.zeros((1, receivers), f32), residual[0]]).reshape(
-        total_steps + 1, receivers // 128, 128
-    )
+    wave = SCALE * ricker(jnp.arange(total_steps, dtype=f32))
 
     smem = pl.BlockSpec(memory_space=pltpu.SMEM)
     vmem = pl.BlockSpec(memory_space=pltpu.VMEM)
@@ -352,36 +462,67 @@
     params = pltpu.CompilerParams(vmem_limit_bytes=VMEM_BYTES)
     l_scratch = [
         pltpu.VMEM(((depth + SHIFT) * parts * SUB, width_y), f32),
-        pltpu.SMEM((3, receivers // 128, 128), f32),
-        pltpu.SemaphoreType.DMA(()),
+        pltpu.VMEM((3, receivers, width_y), f32),
+        pltpu.SemaphoreType.DMA((3, receivers // CHUNK)),
     ]
-    layer_bytes = 4 * plane
+
+    def lane_scratch(layers):
+        rows = layers * parts * SUB
+        return [pltpu.VMEM((rows, PIECES * width_y), jnp.bfloat16), pltpu.VMEM((rows, width_y), f32)]
+
+    block_scratch = [pltpu.VMEM((SPAN, parts, SUB, width_y), f32)] * 4 + lane_scratch(2 * SHIFT)
 
     def cost(layers):
         return pl.CostEstimate(
-            flops=50 * layers * plane, bytes_accessed=6 * layers * layer_bytes, transcendentals=0
+            flops=50 * layers * plane, bytes_accessed=24 * layers * plane, transcendentals=0
         )
 
     f0, f1 = tiled(fwd_prev[0]), tiled(fwd_last[0])
     um, ur = pl.pallas_call(
         first_u_kernel,
         out_shape=(fields(MSG), fields(REST)),
-        in_specs=[smem, smem, vmem, vmem, vmem],
+        in_specs=[smem, smem] + [vmem] * 4,
         out_specs=(vmem, vmem),
+        scratch_shapes=lane_scratch(SHIFT),
         compiler_params=params,
         cost_estimate=cost(SHIFT),
         name="first_u",
-    )(scal_of(total_steps - 1), wave, f0, f1, coef_own)
+    )(scal_of(total_steps - 1), wave, f0, f1, coef_own, weights)
+    u_got = lax.ppermute(um, "slab", up)
+
+    table = pl.pallas_call(
+        table_kernel,
+        out_shape=jax.ShapeDtypeStruct((total_steps, receivers, width_y), f32),
+        in_specs=[smem] + [vmem] * 5,
+        out_specs=anym,
+        scratch_shapes=[
+            pltpu.VMEM((receivers // CHUNK, total_steps, CHUNK), f32),
+            pltpu.VMEM((PIECES * total_steps, receivers), jnp.bfloat16),
+            pltpu.VMEM((CHUNK, CHUNK), f32),
+            pltpu.VMEM((total_steps, CHUNK, width_y), f32),
+            pltpu.SemaphoreType.DMA(()),
+        ],
+        compiler_params=params,
+        cost_estimate=cost(SHIFT),
+        name="rec_table",
+    )(
+        starts,
+        ids.reshape(receivers // CHUNK, CHUNK),
+        rows_of.reshape(receivers // CHUNK, CHUNK),
+        rows_of[:, None],
+        lane[:, None],
+        residual[0],
+    )
     lm, lr, g = pl.pallas_call(
-        functools.partial(first_l_kernel, bits),
+        first_l_kernel,
         out_shape=(fields(MSG), fields(REST), fields(depth + SHIFT)),
-        in_specs=[smem, smem, smem, smem, anym, vmem, vmem],
+        in_specs=[smem, smem, smem, anym, vmem, vmem],
         out_specs=(vmem, vmem, vmem),
         scratch_shapes=l_scratch,
         compiler_params=params,
         cost_estimate=cost(SHIFT),
         name="first_l",
-    )(scal_of(total_steps - 1), rl, ids, starts, res, f0, coef_own)
+    )(scal_of(total_steps - 1), rows_of, starts, table, f0, coef_own)
 
     def u_block(side, n0, own, rest, recv, *vmsg):
         outs = [fields(MSG), fields(REST)]
@@ -389,15 +530,15 @@
             outs.append(fields(MSG))
         outs.append(fields(48))
         return pl.pallas_call(
-            functools.partial(block_kernel, side, False, bits),
+            functools.partial(block_kernel, side, False),
             out_shape=outs,
-            in_specs=[smem, smem] + [vmem] * (4 + len(vmsg)),
+            in_specs=[smem, smem] + [vmem] * (5 + len(vmsg)),
             out_specs=[vmem] * len(outs),
-            scratch_shapes=[pltpu.VMEM((SPAN, parts, SUB, width_y), f32)] * 4,
+            scratch_shapes=block_scratch,
             compiler_params=params,
             cost_estimate=cost(2 * depth),
             name=f"u_block{side}",
-        )(scal_of(n0), wave, own, rest, recv, coef, *vmsg)
+        )(scal_of(n0), wave, own, rest, recv, coef, weights, *vmsg)
 
     def l_block(side, n0, own, rest, recv, vmsg, x, g):
         outs = [fields(MSG), fields(REST)]
@@ -405,15 +546,15 @@
             outs.append(fields(MSG))
         outs.append(fields(depth + SHIFT))
         return pl.pallas_call(
-            functools.partial(block_kernel, side, True, bits),
+            functools.partial(block_kernel, side, True),
             out_shape=outs,
-            in_specs=[smem] * 4 + [anym] + [vmem] * (6 + len(vmsg)),
+            in_specs=[smem] * 3 + [anym] + [vmem] * (7 + len(vmsg)),
             out_specs=[vmem] * len(outs),
-            scratch_shapes=[pltpu.VMEM((SPAN, parts, SUB, width_y), f32)] * 4 + l_scratch,
+            scratch_shapes=block_scratch + l_scratch,
             compiler_params=params,
             cost_estimate=cost(2 * depth),
             name=f"l_block{side}",
-        )(scal_of(n0), rl, ids, starts, res, own, rest, recv, coef, *vmsg, x, g)
+        )(scal_of(n0), rows_of, starts, table, own, rest, recv, coef, weights, *vmsg, x, g)
 
     def two_blocks(i, carry):
         um, ur, u_got, lm, lr, g = carry
@@ -421,21 +562,21 @@
         l_got = lax.ppermute(lm, "slab", up)
         um, ur, uv, x = u_block(0, n0, um, ur, u_got)
         u_got = lax.ppermute(um, "slab", down)
-        lm, lr, lv, g = l_block(0, n0, lm, lr, l_got, (), x, g)
+        lm, lr, lv, g_half = l_block(0, n0, lm, lr, l_got, (), x, g)
         l_got = lax.ppermute(lm, "slab", down)
         um, ur, x = u_block(1, n0 - 2, um, ur, u_got, uv)
         u_got = lax.ppermute(um, "slab", up)
-        lm, lr, g = l_block(1, n0 - 2, lm, lr, l_got, (lv,), x, g)
-        return (um, ur, u_got, lm, lr, g)
-
-    u_got = lax.ppermute(um, "slab", up)
-    um, ur, u_got, lm, lr, g = lax.fori_loop(0, total_steps // 4, two_blocks, (um, ur, u_got, lm, lr, g))
-
+        lm, lr, g = l_block(1, n0 - 2, lm, lr, l_got, (lv,), x, g_half)
+        return (um, ur, u_got, lm, lr, g), g_half
+
+    pairs = total_steps // 4
+    carry = lax.fori_loop(0, pairs - 1, lambda i, c: two_blocks(i, c)[0], (um, ur, u_got, lm, lr, g))
+    (_, _, _, lm, lr, g), g_half = two_blocks(pairs - 1, carry)
+
+    g_right = lax.ppermute(g_half[:SHIFT], "slab", down)
     adjoint_field = untiled(jnp.concatenate([lr[:SHIFT], lm[:SHIFT]], axis=0))[None]
-    g_right = lax.ppermute(g[:SHIFT], "slab", down)
     g = jnp.concatenate([g[SHIFT : 2 * SHIFT], g[2 * SHIFT :] + g_right], axis=0)
-    g = aperture[0].astype(f32) * untiled(g)
-    summed = lax.psum_scatter(g, "shot", scatter_dimension=1, tiled=True)
+    summed = sum_shots(aperture[0].astype(f32) * untiled(g))
     block = width_x // lax.axis_size("shot")
     speed = lax.dynamic_slice_in_dim(velocity, lax.axis_index("shot") * block, block, 1)
     return ((-2.0 / speed) * summed, adjoint_field)

time: 481 us -> 397 us (0.83)
  Pallas kernels: 250 us -> 197 us
  starting transfers between devices: 111 us -> 87.3 us
  local copies, waits for them, and re-layouts: 49 us -> 65.1 us
  between operations: 15.2 us -> 1.9 us
  waiting for transfers between devices: 35.8 us -> 28.6 us
    pallas_call x33 -> x34, Pallas kernels: 248 us -> 195 us  [the longest x16 111 us: l_block(): pl.pallas_call(functools.partial(block_kernel, side, True), out_shape=out...]
    reduce_scatter x1 -> x0, waiting for transfers between devices: 24.8 us -> none  [on_device(): summed = lax.psum_scatter(g, 'shot', scatter_dimension=1, tiled=True)]
    ppermute x8, starting transfers between devices: 40.4 us -> 24.1 us  [two_blocks(): l_got = lax.ppermute(lm, 'slab', up)]
    unnamed x17 -> x46, local copies, waits for them, and re-layouts: 0.1 us -> 16 us
    ppermute x8 -> x7, waiting for transfers between devices: 0.02 us -> 13.3 us  [two_blocks(): u_got = lax.ppermute(um, 'slab', up)]
    ppermute x8 -> x7, starting transfers between devices: 28.5 us -> 16.8 us  [two_blocks(): u_got = lax.ppermute(um, 'slab', up)]
    another operation x0 -> x8, local copies, waits for them, and re-layouts: none -> 6.19 us  [lane_weights(): return jnp.tile(once.astype(jnp.bfloat16), (PIECES, 1))]
    while x128 -> x126, local copies, waits for them, and re-layouts: 43.3 us -> 37.9 us
  transfers between devices with their start and end apart: 36 -> 35, of which waited for: 4 -> 16; matrix products, arithmetic and copies ran while one was open for 2% -> 4% of each run, Pallas kernels for 52% -> 50%
where the time goes in v2:
time: 397 us; the launch traced here: 392 us
  Pallas kernels  197 us (50%)
  starting transfers between devices  87.3 us (22%)
  local copies, waits for them, and re-layouts  65.1 us (16%)
  waiting for transfers between devices  28.6 us (7%)
  other arithmetic  11.2 us (3%)
    pallas_call x16, Pallas kernels, l_block(): pl.pallas_call(functools.partial(block_kernel, side, True), out_shape=out...  111 us
    pallas_call x16, Pallas kernels, u_block(): pl.pallas_call(functools.partial(block_kernel, side, False), out_shape=ou...  71.1 us
    while x126, local copies, waits for them, and re-layouts  37.9 us
    ppermute x8, starting transfers between devices, two_blocks(): l_got = lax.ppermute(lm, 'slab', up)  24.1 us
    ppermute x8, starting transfers between devices, two_blocks(): u_got = lax.ppermute(um, 'slab', down)  20.2 us
    ppermute x7, starting transfers between devices, two_blocks(): u_got = lax.ppermute(um, 'slab', up)  16.8 us
    unnamed x46, local copies, waits for them, and re-layouts  16 us
    ppermute x8, starting transfers between devices, two_blocks(): l_got = lax.ppermute(lm, 'slab', down)  15.3 us
  transfers between devices with their start and end apart: 35, of which 16 were waited for; matrix products, arithmetic and copies ran while one was open for 4% of the time, Pallas kernels for 50%

profile of v2, /device:TPU:12, one launch (start us, length us, event | category | flops | bytes accessed | tf_op | source)
XLA Modules:
  0.0 392.3 jit_solution(6888144790625741673)
XLA Ops:
  10.1 3.5 collective-permute-start.5
  13.7 4.3 %sort.15 = (s32[2048]{0:T(1024)S(1)}, s32[2048]{0:T(1024)S(1)}) sort(s32[2048]{0:T(1024)S(1)} %and_select_fusion, s32[2048]{0:T(1024)S(1)} %iota.34), dimensions={0}, to_apply=%region_0.1 | sort | flops 22528 | bytes 32768 | tf_op jit(solution)/shard_map/sort | solution.py:431
  19.0 10.1 %rec_table.1.table_hbm.refs_3_ = f32[32,2048,128]{2,1,0:T(8,128)S(1)} custom-call(s32[7]{0:T(128)S(1)} %convert_reduce_fusion.starts.refs_2_, s32[8,256]{1,0:T(8,128)S(1)} %reshape.51.ids, s32[8,256]{1,0:T(8,128)S(1)} %reshape.52.rows_l, s32[2048,1]{1,0:T(8,128)S(1)} %copy.17.rows_s, s32[2048,1]{1,0:T(8,128)S(1)} %copy.18.lanes_s, f32[32,2048]{1,0:T(8,128)S(1)} %bitcast.75), custom_call_target="tpu_custom_call" | custom-call | flops 3276800 | bytes 1572864 | tf_op jit(solution)/shard_map/rec_table/pallas_call | solution.py:493
  29.2 3.3 first_l.1
  32.4 8.3 %copy-done.21 = f32[32,2048,128]{2,1,0:T(8,128)} copy-done((f32[32,2048,128]{2,1,0:T(8,128)}, f32[32,2048,128]{2,1,0:T(8,128)S(1)}, u32[]{:S(2)}) %copy-start.21) | copy-done | bytes 33554456
  42.8 299.0 %while.29 = (s32[]{:T(128)}, f32[20,8,8,128]{3,2,1,0:T(8,128)}, f32[12,8,8,128]{3,2,1,0:T(8,128)}, f32[20,8,8,128]{3,2,1,0:T(8,128)}, f32[20,8,8,128]{3,2,1,0:T(...) while((s32[]{:T(128)}, f32[20,8,8,128]{3,2,1,0:T(8,128)}, ...), condition=%wide.region_3.4_spmd.clone.clone, body=%wide.region_2.3_spmd.clone.clone.sunk | while | flops 52429092 | bytes 57803612 | solution.py:573
  45.6 4.2 %u_block0.13 = (f32[20,8,8,128]{3,2,1,0:T(8,128)S(1)}, f32[12,8,8,128]{3,2,1,0:T(8,128)S(1)}, f32[20,8,8,128]{3,2,1,0:T(8,128)S(1)}, f32[48,8,8,128]{3,2,1,0:T(8,128)S(1)}) custom-call(s32[6]{0:T(128)S(1)} %stack.197.refs_0_, f32[32]{0:T(128)S(1)} %multiply_multiply_fusion.3.refs_1_, f32[20,8,8,128]{3,2,1,0:T(8,128)} %get-tuple-element.938.refs_2_, ...), custom_call_target="tpu_custom_call" | custom-call | flops 13107200 | bytes 6291456 | tf_op jit(solution)/shard_map/while/body/eval_jaxpr/u_block0/pallas_call | solution.py:532
  51.4 3.6 collective-permute-start
  57.0 7.1 %l_block0.13 = (f32[20,8,8,128]{3,2,1,0:T(8,128)}, f32[12,8,8,128]{3,2,1,0:T(8,128)S(1)}, f32[20,8,8,128]{3,2,1,0:T(8,128)S(1)}, f32[24,8,8,128]{3,2,1,0:T(8,128)S(1)}) custom-call(s32[6]{0:T(128)S(1)} %stack.197.refs_0_, s32[2048]{0:T(1024)S(1)} %get-tuple-element.971.refs_1_, s32[7]{0:T(128)S(1)} %get-tuple-element.972.refs_2_, ...), custom_call_target="tpu_custom_call" | custom-call | flops 13107200 | bytes 6291456 | tf_op jit(solution)/shard_map/while/body/eval_jaxpr/l_block0/pallas_call | solution.py:548
  66.9 4.7 %u_block1.13 = (f32[20,8,8,128]{3,2,1,0:T(8,128)}, f32[12,8,8,128]{3,2,1,0:T(8,128)}, f32[48,8,8,128]{3,2,1,0:T(8,128)S(1)}) custom-call(s32[6]{0:T(128)S(1)} %stack.196.refs_0_, f32[32]{0:T(128)S(1)} %multiply_multiply_fusion.3.refs_1_, f32[20,8,8,128]{3,2,1,0:T(8,128)S(1)} %get-tuple-element.902.refs_2_, f32[12,8,8,128]{3,2,1,0:T(8,128)S(1)} %copy-done.7, ...), custom_call_target="tpu_custom_call" | custom-call | flops 13107200 | bytes 6291456 | tf_op jit(solution)/shard_map/while/body/eval_jaxpr/u_block1/pallas_call | solution.py:532
  76.3 7.3 %l_block1.13 = (f32[20,8,8,128]{3,2,1,0:T(8,128)}, f32[12,8,8,128]{3,2,1,0:T(8,128)}, f32[24,8,8,128]{3,2,1,0:T(8,128)}) custom-call(s32[6]{0:T(128)S(1)} %stack.196.refs_0_, s32[2048]{0:T(1024)S(1)} %get-tuple-element.971.refs_1_, s32[7]{0:T(128)S(1)} %get-tuple-element.972.refs_2_, f32[32,2048,128]{2,1,0:T(8,128)} %get-tuple-element.973.refs_3_, ...), custom_call_target="tpu_custom_call" | custom-call | flops 13107200 | bytes 6291456 | tf_op jit(solution)/shard_map/while/body/eval_jaxpr/l_block1/pallas_call | solution.py:548
  85.1 3.2 collective-permute-start.2
  89.2 4.2 %u_block0.13 = (f32[20,8,8,128]{3,2,1,0:T(8,128)S(1)}, f32[12,8,8,128]{3,2,1,0:T(8,128)S(1)}, f32[20,8,8,128]{3,2,1,0:T(8,128)S(1)}, f32[48,8,8,128]{3,2,1,0:T(8,128)S(1)}) custom-call(s32[6]{0:T(128)S(1)} %stack.197.refs_0_, f32[32]{0:T(128)S(1)} %multiply_multiply_fusion.3.refs_1_, f32[20,8,8,128]{3,2,1,0:T(8,128)} %get-tuple-element.938.refs_2_, ...), custom_call_target="tpu_custom_call" | custom-call | flops 13107200 | bytes 6291456 | tf_op jit(solution)/shard_map/while/body/eval_jaxpr/u_block0/pallas_call | solution.py:532
  99.3 7.1 %l_block0.13 = (f32[20,8,8,128]{3,2,1,0:T(8,128)}, f32[12,8,8,128]{3,2,1,0:T(8,128)S(1)}, f32[20,8,8,128]{3,2,1,0:T(8,128)S(1)}, f32[24,8,8,128]{3,2,1,0:T(8,128)S(1)}) custom-call(s32[6]{0:T(128)S(1)} %stack.197.refs_0_, s32[2048]{0:T(1024)S(1)} %get-tuple-element.971.refs_1_, s32[7]{0:T(128)S(1)} %get-tuple-element.972.refs_2_, ...), custom_call_target="tpu_custom_call" | custom-call | flops 13107200 | bytes 6291456 | tf_op jit(solution)/shard_map/while/body/eval_jaxpr/l_block0/pallas_call | solution.py:548
  109.2 4.7 %u_block1.13 = (f32[20,8,8,128]{3,2,1,0:T(8,128)}, f32[12,8,8,128]{3,2,1,0:T(8,128)}, f32[48,8,8,128]{3,2,1,0:T(8,128)S(1)}) custom-call(s32[6]{0:T(128)S(1)} %stack.196.refs_0_, f32[32]{0:T(128)S(1)} %multiply_multiply_fusion.3.refs_1_, f32[20,8,8,128]{3,2,1,0:T(8,128)S(1)} %get-tuple-element.902.refs_2_, f32[12,8,8,128]{3,2,1,0:T(8,128)S(1)} %copy-done.7, ...), custom_call_target="tpu_custom_call" | custom-call | flops 13107200 | bytes 6291456 | tf_op jit(solution)/shard_map/while/body/eval_jaxpr/u_block1/pallas_call | solution.py:532
  118.6 7.3 %l_block1.13 = (f32[20,8,8,128]{3,2,1,0:T(8,128)}, f32[12,8,8,128]{3,2,1,0:T(8,128)}, f32[24,8,8,128]{3,2,1,0:T(8,128)}) custom-call(s32[6]{0:T(128)S(1)} %stack.196.refs_0_, s32[2048]{0:T(1024)S(1)} %get-tuple-element.971.refs_1_, s32[7]{0:T(128)S(1)} %get-tuple-element.972.refs_2_, f32[32,2048,128]{2,1,0:T(8,128)} %get-tuple-element.973.refs_3_, ...), custom_call_target="tpu_custom_call" | custom-call | flops 13107200 | bytes 6291456 | tf_op jit(solution)/shard_map/while/body/eval_jaxpr/l_block1/pallas_call | solution.py:548
  127.9 3.2 collective-permute-start.2
  131.9 4.2 %u_block0.13 = (f32[20,8,8,128]{3,2,1,0:T(8,128)S(1)}, f32[12,8,8,128]{3,2,1,0:T(8,128)S(1)}, f32[20,8,8,128]{3,2,1,0:T(8,128)S(1)}, f32[48,8,8,128]{3,2,1,0:T(8,128)S(1)}) custom-call(s32[6]{0:T(128)S(1)} %stack.197.refs_0_, f32[32]{0:T(128)S(1)} %multiply_multiply_fusion.3.refs_1_, f32[20,8,8,128]{3,2,1,0:T(8,128)} %get-tuple-element.938.refs_2_, ...), custom_call_target="tpu_custom_call" | custom-call | flops 13107200 | bytes 6291456 | tf_op jit(solution)/shard_map/while/body/eval_jaxpr/u_block0/pallas_call | solution.py:532
  142.1 7.1 %l_block0.13 = (f32[20,8,8,128]{3,2,1,0:T(8,128)}, f32[12,8,8,128]{3,2,1,0:T(8,128)S(1)}, f32[20,8,8,128]{3,2,1,0:T(8,128)S(1)}, f32[24,8,8,128]{3,2,1,0:T(8,128)S(1)}) custom-call(s32[6]{0:T(128)S(1)} %stack.197.refs_0_, s32[2048]{0:T(1024)S(1)} %get-tuple-element.971.refs_1_, s32[7]{0:T(128)S(1)} %get-tuple-element.972.refs_2_, ...), custom_call_target="tpu_custom_call" | custom-call | flops 13107200 | bytes 6291456 | tf_op jit(solution)/shard_map/while/body/eval_jaxpr/l_block0/pallas_call | solution.py:548
  152.0 4.7 %u_block1.13 = (f32[20,8,8,128]{3,2,1,0:T(8,128)}, f32[12,8,8,128]{3,2,1,0:T(8,128)}, f32[48,8,8,128]{3,2,1,0:T(8,128)S(1)}) custom-call(s32[6]{0:T(128)S(1)} %stack.196.refs_0_, f32[32]{0:T(128)S(1)} %multiply_multiply_fusion.3.refs_1_, f32[20,8,8,128]{3,2,1,0:T(8,128)S(1)} %get-tuple-element.902.refs_2_, f32[12,8,8,128]{3,2,1,0:T(8,128)S(1)} %copy-done.7, ...), custom_call_target="tpu_custom_call" | custom-call | flops 13107200 | bytes 6291456 | tf_op jit(solution)/shard_map/while/body/eval_jaxpr/u_block1/pallas_call | solution.py:532
  161.4 7.3 %l_block1.13 = (f32[20,8,8,128]{3,2,1,0:T(8,128)}, f32[12,8,8,128]{3,2,1,0:T(8,128)}, f32[24,8,8,128]{3,2,1,0:T(8,128)}) custom-call(s32[6]{0:T(128)S(1)} %stack.196.refs_0_, s32[2048]{0:T(1024)S(1)} %get-tuple-element.971.refs_1_, s32[7]{0:T(128)S(1)} %get-tuple-element.972.refs_2_, f32[32,2048,128]{2,1,0:T(8,128)} %get-tuple-element.973.refs_3_, ...), custom_call_target="tpu_custom_call" | custom-call | flops 13107200 | bytes 6291456 | tf_op jit(solution)/shard_map/while/body/eval_jaxpr/l_block1/pallas_call | solution.py:548
  170.7 3.2 collective-permute-start.2
  174.7 4.2 %u_block0.13 = (f32[20,8,8,128]{3,2,1,0:T(8,128)S(1)}, f32[12,8,8,128]{3,2,1,0:T(8,128)S(1)}, f32[20,8,8,128]{3,2,1,0:T(8,128)S(1)}, f32[48,8,8,128]{3,2,1,0:T(8,128)S(1)}) custom-call(s32[6]{0:T(128)S(1)} %stack.197.refs_0_, f32[32]{0:T(128)S(1)} %multiply_multiply_fusion.3.refs_1_, f32[20,8,8,128]{3,2,1,0:T(8,128)} %get-tuple-element.938.refs_2_, ...), custom_call_target="tpu_custom_call" | custom-call | flops 13107200 | bytes 6291456 | tf_op jit(solution)/shard_map/while/body/eval_jaxpr/u_block0/pallas_call | solution.py:532
  184.9 7.1 %l_block0.13 = (f32[20,8,8,128]{3,2,1,0:T(8,128)}, f32[12,8,8,128]{3,2,1,0:T(8,128)S(1)}, f32[20,8,8,128]{3,2,1,0:T(8,128)S(1)}, f32[24,8,8,128]{3,2,1,0:T(8,128)S(1)}) custom-call(s32[6]{0:T(128)S(1)} %stack.197.refs_0_, s32[2048]{0:T(1024)S(1)} %get-tuple-element.971.refs_1_, s32[7]{0:T(128)S(1)} %get-tuple-element.972.refs_2_, ...), custom_call_target="tpu_custom_call" | custom-call | flops 13107200 | bytes 6291456 | tf_op jit(solution)/shard_map/while/body/eval_jaxpr/l_block0/pallas_call | solution.py:548
  194.8 4.7 %u_block1.13 = (f32[20,8,8,128]{3,2,1,0:T(8,128)}, f32[12,8,8,128]{3,2,1,0:T(8,128)}, f32[48,8,8,128]{3,2,1,0:T(8,128)S(1)}) custom-call(s32[6]{0:T(128)S(1)} %stack.196.refs_0_, f32[32]{0:T(128)S(1)} %multiply_multiply_fusion.3.refs_1_, f32[20,8,8,128]{3,2,1,0:T(8,128)S(1)} %get-tuple-element.902.refs_2_, f32[12,8,8,128]{3,2,1,0:T(8,128)S(1)} %copy-done.7, ...), custom_call_target="tpu_custom_call" | custom-call | flops 13107200 | bytes 6291456 | tf_op jit(solution)/shard_map/while/body/eval_jaxpr/u_block1/pallas_call | solution.py:532
  204.2 7.3 %l_block1.13 = (f32[20,8,8,128]{3,2,1,0:T(8,128)}, f32[12,8,8,128]{3,2,1,0:T(8,128)}, f32[24,8,8,128]{3,2,1,0:T(8,128)}) custom-call(s32[6]{0:T(128)S(1)} %stack.196.refs_0_, s32[2048]{0:T(1024)S(1)} %get-tuple-element.971.refs_1_, s32[7]{0:T(128)S(1)} %get-tuple-element.972.refs_2_, f32[32,2048,128]{2,1,0:T(8,128)} %get-tuple-element.973.refs_3_, ...), custom_call_target="tpu_custom_call" | custom-call | flops 13107200 | bytes 6291456 | tf_op jit(solution)/shard_map/while/body/eval_jaxpr/l_block1/pallas_call | solution.py:548
  213.4 3.2 collective-permute-start.2
  217.5 4.2 %u_block0.13 = (f32[20,8,8,128]{3,2,1,0:T(8,128)S(1)}, f32[12,8,8,128]{3,2,1,0:T(8,128)S(1)}, f32[20,8,8,128]{3,2,1,0:T(8,128)S(1)}, f32[48,8,8,128]{3,2,1,0:T(8,128)S(1)}) custom-call(s32[6]{0:T(128)S(1)} %stack.197.refs_0_, f32[32]{0:T(128)S(1)} %multiply_multiply_fusion.3.refs_1_, f32[20,8,8,128]{3,2,1,0:T(8,128)} %get-tuple-element.938.refs_2_, ...), custom_call_target="tpu_custom_call" | custom-call | flops 13107200 | bytes 6291456 | tf_op jit(solution)/shard_map/while/body/eval_jaxpr/u_block0/pallas_call | solution.py:532
  227.7 7.1 %l_block0.13 = (f32[20,8,8,128]{3,2,1,0:T(8,128)}, f32[12,8,8,128]{3,2,1,0:T(8,128)S(1)}, f32[20,8,8,128]{3,2,1,0:T(8,128)S(1)}, f32[24,8,8,128]{3,2,1,0:T(8,128)S(1)}) custom-call(s32[6]{0:T(128)S(1)} %stack.197.refs_0_, s32[2048]{0:T(1024)S(1)} %get-tuple-element.971.refs_1_, s32[7]{0:T(128)S(1)} %get-tuple-element.972.refs_2_, ...), custom_call_target="tpu_custom_call" | custom-call | flops 13107200 | bytes 6291456 | tf_op jit(solution)/shard_map/while/body/eval_jaxpr/l_block0/pallas_call | solution.py:548
  237.5 4.7 %u_block1.13 = (f32[20,8,8,128]{3,2,1,0:T(8,128)}, f32[12,8,8,128]{3,2,1,0:T(8,128)}, f32[48,8,8,128]{3,2,1,0:T(8,128)S(1)}) custom-call(s32[6]{0:T(128)S(1)} %stack.196.refs_0_, f32[32]{0:T(128)S(1)} %multiply_multiply_fusion.3.refs_1_, f32[20,8,8,128]{3,2,1,0:T(8,128)S(1)} %get-tuple-element.902.refs_2_, f32[12,8,8,128]{3,2,1,0:T(8,128)S(1)} %copy-done.7, ...), custom_call_target="tpu_custom_call" | custom-call | flops 13107200 | bytes 6291456 | tf_op jit(solution)/shard_map/while/body/eval_jaxpr/u_block1/pallas_call | solution.py:532
  247.0 7.3 %l_block1.13 = (f32[20,8,8,128]{3,2,1,0:T(8,128)}, f32[12,8,8,128]{3,2,1,0:T(8,128)}, f32[24,8,8,128]{3,2,1,0:T(8,128)}) custom-call(s32[6]{0:T(128)S(1)} %stack.196.refs_0_, s32[2048]{0:T(1024)S(1)} %get-tuple-element.971.refs_1_, s32[7]{0:T(128)S(1)} %get-tuple-element.972.refs_2_, f32[32,2048,128]{2,1,0:T(8,128)} %get-tuple-element.973.refs_3_, ...), custom_call_target="tpu_custom_call" | custom-call | flops 13107200 | bytes 6291456 | tf_op jit(solution)/shard_map/while/body/eval_jaxpr/l_block1/pallas_call | solution.py:548
  256.2 3.2 collective-permute-start.2
  260.3 4.2 %u_block0.13 = (f32[20,8,8,128]{3,2,1,0:T(8,128)S(1)}, f32[12,8,8,128]{3,2,1,0:T(8,128)S(1)}, f32[20,8,8,128]{3,2,1,0:T(8,128)S(1)}, f32[48,8,8,128]{3,2,1,0:T(8,128)S(1)}) custom-call(s32[6]{0:T(128)S(1)} %stack.197.refs_0_, f32[32]{0:T(128)S(1)} %multiply_multiply_fusion.3.refs_1_, f32[20,8,8,128]{3,2,1,0:T(8,128)} %get-tuple-element.938.refs_2_, ...), custom_call_target="tpu_custom_call" | custom-call | flops 13107200 | bytes 6291456 | tf_op jit(solution)/shard_map/while/body/eval_jaxpr/u_block0/pallas_call | solution.py:532
  270.4 7.1 %l_block0.13 = (f32[20,8,8,128]{3,2,1,0:T(8,128)}, f32[12,8,8,128]{3,2,1,0:T(8,128)S(1)}, f32[20,8,8,128]{3,2,1,0:T(8,128)S(1)}, f32[24,8,8,128]{3,2,1,0:T(8,128)S(1)}) custom-call(s32[6]{0:T(128)S(1)} %stack.197.refs_0_, s32[2048]{0:T(1024)S(1)} %get-tuple-element.971.refs_1_, s32[7]{0:T(128)S(1)} %get-tuple-element.972.refs_2_, ...), custom_call_target="tpu_custom_call" | custom-call | flops 13107200 | bytes 6291456 | tf_op jit(solution)/shard_map/while/body/eval_jaxpr/l_block0/pallas_call | solution.py:548
  280.3 4.7 %u_block1.13 = (f32[20,8,8,128]{3,2,1,0:T(8,128)}, f32[12,8,8,128]{3,2,1,0:T(8,128)}, f32[48,8,8,128]{3,2,1,0:T(8,128)S(1)}) custom-call(s32[6]{0:T(128)S(1)} %stack.196.refs_0_, f32[32]{0:T(128)S(1)} %multiply_multiply_fusion.3.refs_1_, f32[20,8,8,128]{3,2,1,0:T(8,128)S(1)} %get-tuple-element.902.refs_2_, f32[12,8,8,128]{3,2,1,0:T(8,128)S(1)} %copy-done.7, ...), custom_call_target="tpu_custom_call" | custom-call | flops 13107200 | bytes 6291456 | tf_op jit(solution)/shard_map/while/body/eval_jaxpr/u_block1/pallas_call | solution.py:532
  289.8 7.3 %l_block1.13 = (f32[20,8,8,128]{3,2,1,0:T(8,128)}, f32[12,8,8,128]{3,2,1,0:T(8,128)}, f32[24,8,8,128]{3,2,1,0:T(8,128)}) custom-call(s32[6]{0:T(128)S(1)} %stack.196.refs_0_, s32[2048]{0:T(1024)S(1)} %get-tuple-element.971.refs_1_, s32[7]{0:T(128)S(1)} %get-tuple-element.972.refs_2_, f32[32,2048,128]{2,1,0:T(8,128)} %get-tuple-element.973.refs_3_, ...), custom_call_target="tpu_custom_call" | custom-call | flops 13107200 | bytes 6291456 | tf_op jit(solution)/shard_map/while/body/eval_jaxpr/l_block1/pallas_call | solution.py:548
  299.0 3.2 collective-permute-start.2
  303.1 4.2 %u_block0.13 = (f32[20,8,8,128]{3,2,1,0:T(8,128)S(1)}, f32[12,8,8,128]{3,2,1,0:T(8,128)S(1)}, f32[20,8,8,128]{3,2,1,0:T(8,128)S(1)}, f32[48,8,8,128]{3,2,1,0:T(8,128)S(1)}) custom-call(s32[6]{0:T(128)S(1)} %stack.197.refs_0_, f32[32]{0:T(128)S(1)} %multiply_multiply_fusion.3.refs_1_, f32[20,8,8,128]{3,2,1,0:T(8,128)} %get-tuple-element.938.refs_2_, ...), custom_call_target="tpu_custom_call" | custom-call | flops 13107200 | bytes 6291456 | tf_op jit(solution)/shard_map/while/body/eval_jaxpr/u_block0/pallas_call | solution.py:532
  313.2 7.1 %l_block0.13 = (f32[20,8,8,128]{3,2,1,0:T(8,128)}, f32[12,8,8,128]{3,2,1,0:T(8,128)S(1)}, f32[20,8,8,128]{3,2,1,0:T(8,128)S(1)}, f32[24,8,8,128]{3,2,1,0:T(8,128)S(1)}) custom-call(s32[6]{0:T(128)S(1)} %stack.197.refs_0_, s32[2048]{0:T(1024)S(1)} %get-tuple-element.971.refs_1_, s32[7]{0:T(128)S(1)} %get-tuple-element.972.refs_2_, ...), custom_call_target="tpu_custom_call" | custom-call | flops 13107200 | bytes 6291456 | tf_op jit(solution)/shard_map/while/body/eval_jaxpr/l_block0/pallas_call | solution.py:548
  323.1 4.7 %u_block1.13 = (f32[20,8,8,128]{3,2,1,0:T(8,128)}, f32[12,8,8,128]{3,2,1,0:T(8,128)}, f32[48,8,8,128]{3,2,1,0:T(8,128)S(1)}) custom-call(s32[6]{0:T(128)S(1)} %stack.196.refs_0_, f32[32]{0:T(128)S(1)} %multiply_multiply_fusion.3.refs_1_, f32[20,8,8,128]{3,2,1,0:T(8,128)S(1)} %get-tuple-element.902.refs_2_, f32[12,8,8,128]{3,2,1,0:T(8,128)S(1)} %copy-done.7, ...), custom_call_target="tpu_custom_call" | custom-call | flops 13107200 | bytes 6291456 | tf_op jit(solution)/shard_map/while/body/eval_jaxpr/u_block1/pallas_call | solution.py:532
  332.5 7.3 %l_block1.13 = (f32[20,8,8,128]{3,2,1,0:T(8,128)}, f32[12,8,8,128]{3,2,1,0:T(8,128)}, f32[24,8,8,128]{3,2,1,0:T(8,128)}) custom-call(s32[6]{0:T(128)S(1)} %stack.196.refs_0_, s32[2048]{0:T(1024)S(1)} %get-tuple-element.971.refs_1_, s32[7]{0:T(128)S(1)} %get-tuple-element.972.refs_2_, f32[32,2048,128]{2,1,0:T(8,128)} %get-tuple-element.973.refs_3_, ...), custom_call_target="tpu_custom_call" | custom-call | flops 13107200 | bytes 6291456 | tf_op jit(solution)/shard_map/while/body/eval_jaxpr/l_block1/pallas_call | solution.py:548
  341.8 3.2 collective-permute-start.6
  345.9 4.5 %u_block0.12 = (f32[20,8,8,128]{3,2,1,0:T(8,128)S(1)}, f32[12,8,8,128]{3,2,1,0:T(8,128)S(1)}, f32[20,8,8,128]{3,2,1,0:T(8,128)S(1)}, f32[48,8,8,128]{3,2,1,0:T(8,128)S(1)}) custom-call(s32[6]{0:T(128)S(1)} %stack.174.refs_0_, f32[32]{0:T(128)S(1)} %multiply_multiply_fusion.1.wave.refs_1_, f32[20,8,8,128]{3,2,1,0:T(8,128)} %get-tuple-element.618.refs_2_, ...), custom_call_target="tpu_custom_call" | custom-call | flops 13107200 | bytes 6291456 | tf_op jit(solution)/shard_map/u_block0/pallas_call | solution.py:532
  356.7 5.6 %l_block0.12 = (f32[20,8,8,128]{3,2,1,0:T(8,128)S(1)}, f32[12,8,8,128]{3,2,1,0:T(8,128)S(1)}, f32[20,8,8,128]{3,2,1,0:T(8,128)S(1)}, f32[24,8,8,128]{3,2,1,0:T(8,128)S(1)}) custom-call(s32[6]{0:T(128)S(1)} %stack.174.refs_0_, s32[2048]{0:T(1024)S(1)} %get-tuple-element.987, s32[7]{0:T(128)S(1)} %get-tuple-element.990, f32[32,2048,128]{2,1,0:T(8,128)} %get-tuple-element.985, ...), custom_call_target="tpu_custom_call" | custom-call | flops 13107200 | bytes 6291456 | tf_op jit(solution)/shard_map/l_block0/pallas_call | solution.py:548
  366.6 4.6 %collective-permute-start.9 = (f32[8,8,8,128]{3,2,1,0:T(8,128)}, f32[8,8,8,128]{3,2,1,0:T(8,128)}, u32[]{:S(2)}, u32[]{:S(2)}) collective-permute-start(f32[8,8,8,128]{3,2,1,0:T(8,128)} %slice.27), channel_id=1, source_target_pairs={{1,0},{2,1},{3,2},{4,3},{5,4},{6,5},{7,6},{8,7},{9,8},{10,9},{11,1... | collective-permute-start | bytes 786440 | tf_op jit(solution)/shard_map/ppermute | solution.py:576
  373.0 4.3 %u_block1.12 = (f32[20,8,8,128]{3,2,1,0:T(8,128)}, f32[12,8,8,128]{3,2,1,0:T(8,128)}, f32[48,8,8,128]{3,2,1,0:T(8,128)S(1)}) custom-call(s32[6]{0:T(128)S(1)} %stack.173.refs_0_, f32[32]{0:T(128)S(1)} %multiply_multiply_fusion.1.wave.refs_1_, f32[20,8,8,128]{3,2,1,0:T(8,128)S(1)} %get-tuple-element.626.refs_2_, f32[12,8,8,128]{3,2,1,0:T(8,128)S(1)} %copy-done.19, ...), custom_call_target="tpu_custom_call" | custom-call | flops 13107200 | bytes 6291456 | tf_op jit(solution)/shard_map/u_block1/pallas_call | solution.py:532
  377.3 4.8 %l_block1.12 = (f32[20,8,8,128]{3,2,1,0:T(8,128)S(1)}, f32[12,8,8,128]{3,2,1,0:T(8,128)S(1)}, f32[24,8,8,128]{3,2,1,0:T(8,128)S(1)}) custom-call(s32[6]{0:T(128)S(1)} %stack.173.refs_0_, s32[2048]{0:T(1024)S(1)} %get-tuple-element.987, s32[7]{0:T(128)S(1)} %get-tuple-element.990, f32[32,2048,128]{2,1,0:T(8,128)} %get-tuple-element.985, ...), custom_call_target="tpu_custom_call" | custom-call | flops 13107200 | bytes 6291456 | tf_op jit(solution)/shard_map/l_block1/pallas_call | solution.py:548
  385.1 6.4 %collective-permute-done.10 = f32[16,32,128]{2,1,0:T(8,128)S(1)} collective-permute-done((f32[16,32,128]{2,1,0:T(8,128)S(1)}, f32[16,32,128]{2,1,0:T(8,128)S(1)}, u32[]{:S(2)}, u32[]{:S(2)}) %collective-permute-start.10) | collective-permute-done | bytes 262176 | tf_op jit(solution)/shard_map/ppermute | solution.py:403
  (293 shorter events, 141.4 us)
Async XLA Ops:
  3.7 10.0 %copy-start.31 = (s32[1,2048]{1,0:T(1,128)S(1)}, s32[1,2048]{1,0:T(1,128)}, u32[]{:S(2)}) copy-start(s32[1,2048]{1,0:T(1,128)} %param.13) | copy-start | bytes 24580
  7.4 11.7 %copy-start.20 = (f32[1,32,2048]{2,1,0:T(8,128)S(1)}, f32[1,32,2048]{2,1,0:T(8,128)}, u32[]{:S(2)}) copy-start(f32[1,32,2048]{2,1,0:T(8,128)} %param.15) | copy-start | bytes 786436
  7.4 35.4 %collective-permute-start.4 = (f32[20,8,8,128]{3,2,1,0:T(8,128)}, f32[20,8,8,128]{3,2,1,0:T(8,128)}, u32[]{:S(2)}, u32[]{:S(2)}) collective-permute-start(f32[20,8,8,128]{3,2,1,0:T(8,128)} %get-tuple-element.917), channel_id=1, source_target_pairs={{0,1},{1,2},{2,3},{3,4},{4,5},{5,6},{6,7},{7,8},{8,9},{9,10},{10,1... | collective-permute-start | bytes 1966088 | tf_op jit(solution)/shard_map/ppermute | solution.py:491
  10.1 30.6 %collective-permute-start.5 = (f32[8,64,128]{2,1,0:T(8,128)}, f32[8,64,128]{2,1,0:T(8,128)}, u32[]{:S(2)}, u32[]{:S(2)}) collective-permute-start(f32[8,64,128]{2,1,0:T(8,128)} %slice.24), channel_id=1, source_target_pairs={{0,1},{1,2},{2,3},{3,4},{4,5},{5,6},{6,7},{7,8},{8,9},{9,10},{10,1... | collective-permute-start | bytes 786440 | tf_op jit(solution)/shard_map/ppermute | solution.py:421
  29.2 11.6 %copy-start.21 = (f32[32,2048,128]{2,1,0:T(8,128)}, f32[32,2048,128]{2,1,0:T(8,128)S(1)}, u32[]{:S(2)}) copy-start(f32[32,2048,128]{2,1,0:T(8,128)S(1)} %rec_table.1.table_hbm.refs_3_) | copy-start | bytes 100663296
  42.8 12.3 %collective-permute-start.2 = (f32[20,8,8,128]{3,2,1,0:T(8,128)}, f32[20,8,8,128]{3,2,1,0:T(8,128)S(1)}, u32[]{:S(2)}, u32[]{:S(2)}) collective-permute-start(f32[20,8,8,128]{3,2,1,0:T(8,128)} %get-tuple-element.941.refs_4_), channel_id=1, source_target_pairs={{0,1},{1,2},{2,3},{3,4},{4,5},{5,6},{6,7},{7,8},{8,9},{9,10},{10,1... | collective-permute-start | bytes 1966088 | tf_op jit(solution)/shard_map/while/body/eval_jaxpr/ppermute | solution.py:562
  51.4 15.5 %collective-permute-start = (f32[20,8,8,128]{3,2,1,0:T(8,128)S(1)}, f32[20,8,8,128]{3,2,1,0:T(8,128)}, u32[]{:S(2)}, u32[]{:S(2)}) collective-permute-start(f32[20,8,8,128]{3,2,1,0:T(8,128)S(1)} %get-tuple-element.902.refs_2_), channel_id=1, source_target_pairs={{1,0},{2,1},{3,2},{4,3},{5,4},{6,5},{7,6},{8,7},{9,8},{10,9},{11,1... | collective-permute-start | bytes 1966088 | tf_op jit(solution)/shard_map/while/body/eval_jaxpr/ppermute | solution.py:564
  57.0 9.9 %copy-start.22 = (f32[24,8,8,128]{3,2,1,0:T(8,128)S(1)}, f32[24,8,8,128]{3,2,1,0:T(8,128)}, u32[]{:S(2)}) copy-start(f32[24,8,8,128]{3,2,1,0:T(8,128)} %get-tuple-element.970.refs_5_.refs_7_) | copy-start | bytes 2359300 | tf_op jit(solution)/shard_map/while
  64.9 10.3 %collective-permute-start.3 = (f32[20,8,8,128]{3,2,1,0:T(8,128)}, f32[20,8,8,128]{3,2,1,0:T(8,128)}, u32[]{:S(2)}, u32[]{:S(2)}) collective-permute-start(f32[20,8,8,128]{3,2,1,0:T(8,128)} %get-tuple-element.908.refs_4_), channel_id=1, source_target_pairs={{1,0},{2,1},{3,2},{4,3},{5,4},{6,5},{7,6},{8,7},{9,8},{10,9},{11,1... | collective-permute-start | bytes 1966088 | tf_op jit(solution)/shard_map/while/body/eval_jaxpr/ppermute | solution.py:566
  71.6 13.5 %collective-permute-start.1 = (f32[20,8,8,128]{3,2,1,0:T(8,128)}, f32[20,8,8,128]{3,2,1,0:T(8,128)}, u32[]{:S(2)}, u32[]{:S(2)}) collective-permute-start(f32[20,8,8,128]{3,2,1,0:T(8,128)} %get-tuple-element.959), channel_id=1, source_target_pairs={{0,1},{1,2},{2,3},{3,4},{4,5},{5,6},{6,7},{7,8},{8,9},{9,10},{10,1... | collective-permute-start | bytes 1966088 | tf_op jit(solution)/shard_map/while/body/eval_jaxpr/ppermute | solution.py:568
  85.1 12.3 %collective-permute-start.2 = (f32[20,8,8,128]{3,2,1,0:T(8,128)}, f32[20,8,8,128]{3,2,1,0:T(8,128)S(1)}, u32[]{:S(2)}, u32[]{:S(2)}) collective-permute-start(f32[20,8,8,128]{3,2,1,0:T(8,128)} %get-tuple-element.941.refs_4_), channel_id=1, source_target_pairs={{0,1},{1,2},{2,3},{3,4},{4,5},{5,6},{6,7},{7,8},{8,9},{9,10},{10,1... | collective-permute-start | bytes 1966088 | tf_op jit(solution)/shard_map/while/body/eval_jaxpr/ppermute | solution.py:562
  94.9 14.2 %collective-permute-start = (f32[20,8,8,128]{3,2,1,0:T(8,128)S(1)}, f32[20,8,8,128]{3,2,1,0:T(8,128)}, u32[]{:S(2)}, u32[]{:S(2)}) collective-permute-start(f32[20,8,8,128]{3,2,1,0:T(8,128)S(1)} %get-tuple-element.902.refs_2_), channel_id=1, source_target_pairs={{1,0},{2,1},{3,2},{4,3},{5,4},{6,5},{7,6},{8,7},{9,8},{10,9},{11,1... | collective-permute-start | bytes 1966088 | tf_op jit(solution)/shard_map/while/body/eval_jaxpr/ppermute | solution.py:564
  99.3 9.8 %copy-start.7 = (f32[12,8,8,128]{3,2,1,0:T(8,128)S(1)}, f32[12,8,8,128]{3,2,1,0:T(8,128)}, u32[]{:S(2)}) copy-start(f32[12,8,8,128]{3,2,1,0:T(8,128)} %copy-done.6) | copy-start | bytes 1179652 | tf_op jit(solution)/shard_map/while
  99.3 9.9 %copy-start.22 = (f32[24,8,8,128]{3,2,1,0:T(8,128)S(1)}, f32[24,8,8,128]{3,2,1,0:T(8,128)}, u32[]{:S(2)}) copy-start(f32[24,8,8,128]{3,2,1,0:T(8,128)} %get-tuple-element.970.refs_5_.refs_7_) | copy-start | bytes 2359300 | tf_op jit(solution)/shard_map/while
  107.2 10.3 %collective-permute-start.3 = (f32[20,8,8,128]{3,2,1,0:T(8,128)}, f32[20,8,8,128]{3,2,1,0:T(8,128)}, u32[]{:S(2)}, u32[]{:S(2)}) collective-permute-start(f32[20,8,8,128]{3,2,1,0:T(8,128)} %get-tuple-element.908.refs_4_), channel_id=1, source_target_pairs={{1,0},{2,1},{3,2},{4,3},{5,4},{6,5},{7,6},{8,7},{9,8},{10,9},{11,1... | collective-permute-start | bytes 1966088 | tf_op jit(solution)/shard_map/while/body/eval_jaxpr/ppermute | solution.py:566
  113.9 13.9 %collective-permute-start.1 = (f32[20,8,8,128]{3,2,1,0:T(8,128)}, f32[20,8,8,128]{3,2,1,0:T(8,128)}, u32[]{:S(2)}, u32[]{:S(2)}) collective-permute-start(f32[20,8,8,128]{3,2,1,0:T(8,128)} %get-tuple-element.959), channel_id=1, source_target_pairs={{0,1},{1,2},{2,3},{3,4},{4,5},{5,6},{6,7},{7,8},{8,9},{9,10},{10,1... | collective-permute-start | bytes 1966088 | tf_op jit(solution)/shard_map/while/body/eval_jaxpr/ppermute | solution.py:568
  127.9 12.3 %collective-permute-start.2 = (f32[20,8,8,128]{3,2,1,0:T(8,128)}, f32[20,8,8,128]{3,2,1,0:T(8,128)S(1)}, u32[]{:S(2)}, u32[]{:S(2)}) collective-permute-start(f32[20,8,8,128]{3,2,1,0:T(8,128)} %get-tuple-element.941.refs_4_), channel_id=1, source_target_pairs={{0,1},{1,2},{2,3},{3,4},{4,5},{5,6},{6,7},{7,8},{8,9},{9,10},{10,1... | collective-permute-start | bytes 1966088 | tf_op jit(solution)/shard_map/while/body/eval_jaxpr/ppermute | solution.py:562
  137.7 14.2 %collective-permute-start = (f32[20,8,8,128]{3,2,1,0:T(8,128)S(1)}, f32[20,8,8,128]{3,2,1,0:T(8,128)}, u32[]{:S(2)}, u32[]{:S(2)}) collective-permute-start(f32[20,8,8,128]{3,2,1,0:T(8,128)S(1)} %get-tuple-element.902.refs_2_), channel_id=1, source_target_pairs={{1,0},{2,1},{3,2},{4,3},{5,4},{6,5},{7,6},{8,7},{9,8},{10,9},{11,1... | collective-permute-start | bytes 1966088 | tf_op jit(solution)/shard_map/while/body/eval_jaxpr/ppermute | solution.py:564
  142.1 9.8 %copy-start.7 = (f32[12,8,8,128]{3,2,1,0:T(8,128)S(1)}, f32[12,8,8,128]{3,2,1,0:T(8,128)}, u32[]{:S(2)}) copy-start(f32[12,8,8,128]{3,2,1,0:T(8,128)} %copy-done.6) | copy-start | bytes 1179652 | tf_op jit(solution)/shard_map/while
  142.1 9.9 %copy-start.22 = (f32[24,8,8,128]{3,2,1,0:T(8,128)S(1)}, f32[24,8,8,128]{3,2,1,0:T(8,128)}, u32[]{:S(2)}) copy-start(f32[24,8,8,128]{3,2,1,0:T(8,128)} %get-tuple-element.970.refs_5_.refs_7_) | copy-start | bytes 2359300 | tf_op jit(solution)/shard_map/while
  150.0 10.3 %collective-permute-start.3 = (f32[20,8,8,128]{3,2,1,0:T(8,128)}, f32[20,8,8,128]{3,2,1,0:T(8,128)}, u32[]{:S(2)}, u32[]{:S(2)}) collective-permute-start(f32[20,8,8,128]{3,2,1,0:T(8,128)} %get-tuple-element.908.refs_4_), channel_id=1, source_target_pairs={{1,0},{2,1},{3,2},{4,3},{5,4},{6,5},{7,6},{8,7},{9,8},{10,9},{11,1... | collective-permute-start | bytes 1966088 | tf_op jit(solution)/shard_map/while/body/eval_jaxpr/ppermute | solution.py:566
  156.7 13.9 %collective-permute-start.1 = (f32[20,8,8,128]{3,2,1,0:T(8,128)}, f32[20,8,8,128]{3,2,1,0:T(8,128)}, u32[]{:S(2)}, u32[]{:S(2)}) collective-permute-start(f32[20,8,8,128]{3,2,1,0:T(8,128)} %get-tuple-element.959), channel_id=1, source_target_pairs={{0,1},{1,2},{2,3},{3,4},{4,5},{5,6},{6,7},{7,8},{8,9},{9,10},{10,1... | collective-permute-start | bytes 1966088 | tf_op jit(solution)/shard_map/while/body/eval_jaxpr/ppermute | solution.py:568
  170.7 12.3 %collective-permute-start.2 = (f32[20,8,8,128]{3,2,1,0:T(8,128)}, f32[20,8,8,128]{3,2,1,0:T(8,128)S(1)}, u32[]{:S(2)}, u32[]{:S(2)}) collective-permute-start(f32[20,8,8,128]{3,2,1,0:T(8,128)} %get-tuple-element.941.refs_4_), channel_id=1, source_target_pairs={{0,1},{1,2},{2,3},{3,4},{4,5},{5,6},{6,7},{7,8},{8,9},{9,10},{10,1... | collective-permute-start | bytes 1966088 | tf_op jit(solution)/shard_map/while/body/eval_jaxpr/ppermute | solution.py:562
  180.5 14.2 %collective-permute-start = (f32[20,8,8,128]{3,2,1,0:T(8,128)S(1)}, f32[20,8,8,128]{3,2,1,0:T(8,128)}, u32[]{:S(2)}, u32[]{:S(2)}) collective-permute-start(f32[20,8,8,128]{3,2,1,0:T(8,128)S(1)} %get-tuple-element.902.refs_2_), channel_id=1, source_target_pairs={{1,0},{2,1},{3,2},{4,3},{5,4},{6,5},{7,6},{8,7},{9,8},{10,9},{11,1... | collective-permute-start | bytes 1966088 | tf_op jit(solution)/shard_map/while/body/eval_jaxpr/ppermute | solution.py:564
  184.9 9.9 %copy-start.22 = (f32[24,8,8,128]{3,2,1,0:T(8,128)S(1)}, f32[24,8,8,128]{3,2,1,0:T(8,128)}, u32[]{:S(2)}) copy-start(f32[24,8,8,128]{3,2,1,0:T(8,128)} %get-tuple-element.970.refs_5_.refs_7_) | copy-start | bytes 2359300 | tf_op jit(solution)/shard_map/while
  192.8 10.3 %collective-permute-start.3 = (f32[20,8,8,128]{3,2,1,0:T(8,128)}, f32[20,8,8,128]{3,2,1,0:T(8,128)}, u32[]{:S(2)}, u32[]{:S(2)}) collective-permute-start(f32[20,8,8,128]{3,2,1,0:T(8,128)} %get-tuple-element.908.refs_4_), channel_id=1, source_target_pairs={{1,0},{2,1},{3,2},{4,3},{5,4},{6,5},{7,6},{8,7},{9,8},{10,9},{11,1... | collective-permute-start | bytes 1966088 | tf_op jit(solution)/shard_map/while/body/eval_jaxpr/ppermute | solution.py:566
  199.5 13.9 %collective-permute-start.1 = (f32[20,8,8,128]{3,2,1,0:T(8,128)}, f32[20,8,8,128]{3,2,1,0:T(8,128)}, u32[]{:S(2)}, u32[]{:S(2)}) collective-permute-start(f32[20,8,8,128]{3,2,1,0:T(8,128)} %get-tuple-element.959), channel_id=1, source_target_pairs={{0,1},{1,2},{2,3},{3,4},{4,5},{5,6},{6,7},{7,8},{8,9},{9,10},{10,1... | collective-permute-start | bytes 1966088 | tf_op jit(solution)/shard_map/while/body/eval_jaxpr/ppermute | solution.py:568
  213.4 12.3 %collective-permute-start.2 = (f32[20,8,8,128]{3,2,1,0:T(8,128)}, f32[20,8,8,128]{3,2,1,0:T(8,128)S(1)}, u32[]{:S(2)}, u32[]{:S(2)}) collective-permute-start(f32[20,8,8,128]{3,2,1,0:T(8,128)} %get-tuple-element.941.refs_4_), channel_id=1, source_target_pairs={{0,1},{1,2},{2,3},{3,4},{4,5},{5,6},{6,7},{7,8},{8,9},{9,10},{10,1... | collective-permute-start | bytes 1966088 | tf_op jit(solution)/shard_map/while/body/eval_jaxpr/ppermute | solution.py:562
  223.3 14.2 %collective-permute-start = (f32[20,8,8,128]{3,2,1,0:T(8,128)S(1)}, f32[20,8,8,128]{3,2,1,0:T(8,128)}, u32[]{:S(2)}, u32[]{:S(2)}) collective-permute-start(f32[20,8,8,128]{3,2,1,0:T(8,128)S(1)} %get-tuple-element.902.refs_2_), channel_id=1, source_target_pairs={{1,0},{2,1},{3,2},{4,3},{5,4},{6,5},{7,6},{8,7},{9,8},{10,9},{11,1... | collective-permute-start | bytes 1966088 | tf_op jit(solution)/shard_map/while/body/eval_jaxpr/ppermute | solution.py:564
  227.7 9.9 %copy-start.22 = (f32[24,8,8,128]{3,2,1,0:T(8,128)S(1)}, f32[24,8,8,128]{3,2,1,0:T(8,128)}, u32[]{:S(2)}) copy-start(f32[24,8,8,128]{3,2,1,0:T(8,128)} %get-tuple-element.970.refs_5_.refs_7_) | copy-start | bytes 2359300 | tf_op jit(solution)/shard_map/while
  235.6 10.3 %collective-permute-start.3 = (f32[20,8,8,128]{3,2,1,0:T(8,128)}, f32[20,8,8,128]{3,2,1,0:T(8,128)}, u32[]{:S(2)}, u32[]{:S(2)}) collective-permute-start(f32[20,8,8,128]{3,2,1,0:T(8,128)} %get-tuple-element.908.refs_4_), channel_id=1, source_target_pairs={{1,0},{2,1},{3,2},{4,3},{5,4},{6,5},{7,6},{8,7},{9,8},{10,9},{11,1... | collective-permute-start | bytes 1966088 | tf_op jit(solution)/shard_map/while/body/eval_jaxpr/ppermute | solution.py:566
  242.3 13.9 %collective-permute-start.1 = (f32[20,8,8,128]{3,2,1,0:T(8,128)}, f32[20,8,8,128]{3,2,1,0:T(8,128)}, u32[]{:S(2)}, u32[]{:S(2)}) collective-permute-start(f32[20,8,8,128]{3,2,1,0:T(8,128)} %get-tuple-element.959), channel_id=1, source_target_pairs={{0,1},{1,2},{2,3},{3,4},{4,5},{5,6},{6,7},{7,8},{8,9},{9,10},{10,1... | collective-permute-start | bytes 1966088 | tf_op jit(solution)/shard_map/while/body/eval_jaxpr/ppermute | solution.py:568
  256.2 12.3 %collective-permute-start.2 = (f32[20,8,8,128]{3,2,1,0:T(8,128)}, f32[20,8,8,128]{3,2,1,0:T(8,128)S(1)}, u32[]{:S(2)}, u32[]{:S(2)}) collective-permute-start(f32[20,8,8,128]{3,2,1,0:T(8,128)} %get-tuple-element.941.refs_4_), channel_id=1, source_target_pairs={{0,1},{1,2},{2,3},{3,4},{4,5},{5,6},{6,7},{7,8},{8,9},{9,10},{10,1... | collective-permute-start | bytes 1966088 | tf_op jit(solution)/shard_map/while/body/eval_jaxpr/ppermute | solution.py:562
  266.1 14.2 %collective-permute-start = (f32[20,8,8,128]{3,2,1,0:T(8,128)S(1)}, f32[20,8,8,128]{3,2,1,0:T(8,128)}, u32[]{:S(2)}, u32[]{:S(2)}) collective-permute-start(f32[20,8,8,128]{3,2,1,0:T(8,128)S(1)} %get-tuple-element.902.refs_2_), channel_id=1, source_target_pairs={{1,0},{2,1},{3,2},{4,3},{5,4},{6,5},{7,6},{8,7},{9,8},{10,9},{11,1... | collective-permute-start | bytes 1966088 | tf_op jit(solution)/shard_map/while/body/eval_jaxpr/ppermute | solution.py:564
  270.4 9.9 %copy-start.22 = (f32[24,8,8,128]{3,2,1,0:T(8,128)S(1)}, f32[24,8,8,128]{3,2,1,0:T(8,128)}, u32[]{:S(2)}) copy-start(f32[24,8,8,128]{3,2,1,0:T(8,128)} %get-tuple-element.970.refs_5_.refs_7_) | copy-start | bytes 2359300 | tf_op jit(solution)/shard_map/while
  278.4 10.3 %collective-permute-start.3 = (f32[20,8,8,128]{3,2,1,0:T(8,128)}, f32[20,8,8,128]{3,2,1,0:T(8,128)}, u32[]{:S(2)}, u32[]{:S(2)}) collective-permute-start(f32[20,8,8,128]{3,2,1,0:T(8,128)} %get-tuple-element.908.refs_4_), channel_id=1, source_target_pairs={{1,0},{2,1},{3,2},{4,3},{5,4},{6,5},{7,6},{8,7},{9,8},{10,9},{11,1... | collective-permute-start | bytes 1966088 | tf_op jit(solution)/shard_map/while/body/eval_jaxpr/ppermute | solution.py:566
  285.0 13.9 %collective-permute-start.1 = (f32[20,8,8,128]{3,2,1,0:T(8,128)}, f32[20,8,8,128]{3,2,1,0:T(8,128)}, u32[]{:S(2)}, u32[]{:S(2)}) collective-permute-start(f32[20,8,8,128]{3,2,1,0:T(8,128)} %get-tuple-element.959), channel_id=1, source_target_pairs={{0,1},{1,2},{2,3},{3,4},{4,5},{5,6},{6,7},{7,8},{8,9},{9,10},{10,1... | collective-permute-start | bytes 1966088 | tf_op jit(solution)/shard_map/while/body/eval_jaxpr/ppermute | solution.py:568
  299.0 12.3 %collective-permute-start.2 = (f32[20,8,8,128]{3,2,1,0:T(8,128)}, f32[20,8,8,128]{3,2,1,0:T(8,128)S(1)}, u32[]{:S(2)}, u32[]{:S(2)}) collective-permute-start(f32[20,8,8,128]{3,2,1,0:T(8,128)} %get-tuple-element.941.refs_4_), channel_id=1, source_target_pairs={{0,1},{1,2},{2,3},{3,4},{4,5},{5,6},{6,7},{7,8},{8,9},{9,10},{10,1... | collective-permute-start | bytes 1966088 | tf_op jit(solution)/shard_map/while/body/eval_jaxpr/ppermute | solution.py:562
  308.8 14.2 %collective-permute-start = (f32[20,8,8,128]{3,2,1,0:T(8,128)S(1)}, f32[20,8,8,128]{3,2,1,0:T(8,128)}, u32[]{:S(2)}, u32[]{:S(2)}) collective-permute-start(f32[20,8,8,128]{3,2,1,0:T(8,128)S(1)} %get-tuple-element.902.refs_2_), channel_id=1, source_target_pairs={{1,0},{2,1},{3,2},{4,3},{5,4},{6,5},{7,6},{8,7},{9,8},{10,9},{11,1... | collective-permute-start | bytes 1966088 | tf_op jit(solution)/shard_map/while/body/eval_jaxpr/ppermute | solution.py:564
  313.2 9.9 %copy-start.22 = (f32[24,8,8,128]{3,2,1,0:T(8,128)S(1)}, f32[24,8,8,128]{3,2,1,0:T(8,128)}, u32[]{:S(2)}) copy-start(f32[24,8,8,128]{3,2,1,0:T(8,128)} %get-tuple-element.970.refs_5_.refs_7_) | copy-start | bytes 2359300 | tf_op jit(solution)/shard_map/while
  321.1 10.3 %collective-permute-start.3 = (f32[20,8,8,128]{3,2,1,0:T(8,128)}, f32[20,8,8,128]{3,2,1,0:T(8,128)}, u32[]{:S(2)}, u32[]{:S(2)}) collective-permute-start(f32[20,8,8,128]{3,2,1,0:T(8,128)} %get-tuple-element.908.refs_4_), channel_id=1, source_target_pairs={{1,0},{2,1},{3,2},{4,3},{5,4},{6,5},{7,6},{8,7},{9,8},{10,9},{11,1... | collective-permute-start | bytes 1966088 | tf_op jit(solution)/shard_map/while/body/eval_jaxpr/ppermute | solution.py:566
  327.8 13.9 %collective-permute-start.1 = (f32[20,8,8,128]{3,2,1,0:T(8,128)}, f32[20,8,8,128]{3,2,1,0:T(8,128)}, u32[]{:S(2)}, u32[]{:S(2)}) collective-permute-start(f32[20,8,8,128]{3,2,1,0:T(8,128)} %get-tuple-element.959), channel_id=1, source_target_pairs={{0,1},{1,2},{2,3},{3,4},{4,5},{5,6},{6,7},{7,8},{8,9},{9,10},{10,1... | collective-permute-start | bytes 1966088 | tf_op jit(solution)/shard_map/while/body/eval_jaxpr/ppermute | solution.py:568
  341.8 12.1 %collective-permute-start.6 = (f32[20,8,8,128]{3,2,1,0:T(8,128)}, f32[20,8,8,128]{3,2,1,0:T(8,128)S(1)}, u32[]{:S(2)}, u32[]{:S(2)}) collective-permute-start(f32[20,8,8,128]{3,2,1,0:T(8,128)} %get-tuple-element.616.refs_4_), channel_id=1, source_target_pairs={{0,1},{1,2},{2,3},{3,4},{4,5},{5,6},{6,7},{7,8},{8,9},{9,10},{10,1... | collective-permute-start | bytes 1966088 | tf_op jit(solution)/shard_map/ppermute | solution.py:562
  351.2 20.8 %collective-permute-start.8 = (f32[20,8,8,128]{3,2,1,0:T(8,128)S(1)}, f32[20,8,8,128]{3,2,1,0:T(8,128)S(1)}, u32[]{:S(2)}, u32[]{:S(2)}) collective-permute-start(f32[20,8,8,128]{3,2,1,0:T(8,128)S(1)} %get-tuple-element.626.refs_2_), channel_id=1, source_target_pairs={{1,0},{2,1},{3,2},{4,3},{5,4},{6,5},{7,6},{8,7},{9,8},{10,9},{11,1... | collective-permute-start | bytes 1966088 | tf_op jit(solution)/shard_map/ppermute | solution.py:564
  356.7 15.3 %copy-start.11 = (bf16[3,128,128]{2,1,0:T(8,128)(2,1)S(1)}, bf16[3,128,128]{2,1,0:T(8,128)(2,1)}, u32[]{:S(2)}) copy-start(bf16[3,128,128]{2,1,0:T(8,128)(2,1)} %copy-done.8) | copy-start | bytes 294916
  363.9 13.4 %collective-permute-start.7 = (f32[20,8,8,128]{3,2,1,0:T(8,128)S(1)}, f32[20,8,8,128]{3,2,1,0:T(8,128)}, u32[]{:S(2)}, u32[]{:S(2)}) collective-permute-start(f32[20,8,8,128]{3,2,1,0:T(8,128)S(1)} %get-tuple-element.623.refs_4_), channel_id=1, source_target_pairs={{1,0},{2,1},{3,2},{4,3},{5,4},{6,5},{7,6},{8,7},{9,8},{10,9},{11,1... | collective-permute-start | bytes 1966088 | tf_op jit(solution)/shard_map/ppermute | solution.py:566
  366.6 15.6 %collective-permute-start.9 = (f32[8,8,8,128]{3,2,1,0:T(8,128)}, f32[8,8,8,128]{3,2,1,0:T(8,128)}, u32[]{:S(2)}, u32[]{:S(2)}) collective-permute-start(f32[8,8,8,128]{3,2,1,0:T(8,128)} %slice.27), channel_id=1, source_target_pairs={{1,0},{2,1},{3,2},{4,3},{5,4},{6,5},{7,6},{8,7},{9,8},{10,9},{11,1... | collective-permute-start | bytes 786440 | tf_op jit(solution)/shard_map/ppermute | solution.py:576
  383.4 8.1 %collective-permute-start.10 = (f32[16,32,128]{2,1,0:T(8,128)S(1)}, f32[16,32,128]{2,1,0:T(8,128)S(1)}, u32[]{:S(2)}, u32[]{:S(2)}) collective-permute-start(f32[16,32,128]{2,1,0:T(8,128)S(1)} %slice_select_fusion), channel_id=1, source_target_pairs={{0,16},{16,0},{1,17},{17,1},{2,18},{18,2},{3,19},{19,3},{4,20},{20... | collective-permute-start | bytes 786440 | tf_op jit(solution)/shard_map/ppermute | solution.py:403
  (73 other events, 222.0 us)
